TPU v7x, 128 devices: a whole 4x4x4 slice. The times are simulated.
128 devices in a mesh: dp: 16 (over z, x), enc: 8 (over y, core).
Axes of the slice: x: 4, y: 4, z: 4, core: 2. Of those that a mesh axis runs over, the one named last changes fastest.
Arguments:
- chars: int32 [786432, 50], P('dp'), may hold values from 0 to 261
- char_table: bfloat16 [262, 16], replicated, may hold values from -6 to 6
- conv_weight: bfloat16 [7, 16, 2048], P(None, None, 'enc'), may hold values from -0.75 to 0.75
- conv_bias: float32 [2048], P('enc'), may hold values from -3 to 3
- hw_weight: bfloat16 [2, 2048, 2, 2048], P(None, None, None, 'enc'), may hold values from -0.125 to 0.125
- hw_bias: float32 [2, 2, 2048], P(None, None, 'enc'), may hold values from -4 to 4
- proj_weight: bfloat16 [2048, 512], P('enc'), may hold values from -0.125 to 0.125
- proj_bias: float32 [512], P('enc'), may hold values from -3 to 3
- owner_types: int32 [16384], P('dp'), may hold values from 0 to 49151, as said below
- requests: int32 [16, 16, 256], P('dp'), may hold values from -1 to 1023, as said below
- tok_slot: int32 [131072], P('dp'), may hold values from 0 to 4095, as said below
- d_tokens: bfloat16 [131072, 512], P('dp', 'enc'), may hold values from -0.59765625 to 0.59765625
Outputs:
- token_vectors: bfloat16 [131072, 512], P('dp', 'enc')
- d_features: bfloat16 [16384, 2048], P('dp', 'enc')
- d_highway: float32 [2, 2048, 2, 2048], P(None, 'dp', None, 'enc')
- d_projection: float32 [2048, 512], P('enc', 'dp')
Inputs may be any that keep to these rules, and one draw needn't show every extreme that they name: `owner_types`: entries o * 1024 to (o + 1) * 1024 - 1 are distinct rows of owner o's 49152 rows of chars; every owner's list holds its first and its last row. `requests`: list (r, o) holds 64 to 256 distinct positions of owner o's unique list, then -1 entries. Every position of every owner's list is asked for by some replica. In every draw one owner receives full lists (256 positions) from every replica, and some list is not full. `tok_slot`: token t of replica r names a slot o * 256 + k with requests[r, o, k] >= 0; every such slot is named by at least one token of replica r.
All inputs are finite; a program needn't handle non-finite values.
Results may differ from a plain program's by a relative error of at most 0.015.
Values may be sent and summed in bfloat16 or wider, within the bound.
A program may use at most 192 MiB of HBM per device.

v0:
```python
import math

import jax
import jax.numpy as jnp
from jax import lax
from jax.sharding import PartitionSpec as P


def filter_widths(filter_index, total_filters):
    width = jnp.ones(filter_index.shape, jnp.int32)
    for share in (1, 2, 4, 8, 16, 32):
        width = width + (filter_index >= share * total_filters // 64).astype(jnp.int32)
    return width


def per_device(
    chars,
    char_table,
    conv_weight,
    conv_bias,
    hw_weight,
    hw_bias,
    proj_weight,
    proj_bias,
    owner_types,
    requests,
    tok_slot,
    d_tokens,
):
    taps, embed_width, local_filters = conv_weight.shape
    layers = hw_weight.shape[0]
    total_filters = hw_weight.shape[1]
    length = chars.shape[1]
    alphabet = char_table.shape[0]
    unique_rows = owner_types.shape[0]
    filter_index = lax.axis_index("enc") * local_filters + jnp.arange(
        local_filters, dtype=jnp.int32
    )
    width = filter_widths(filter_index, total_filters)
    tap_mask = jnp.arange(taps + 1, dtype=jnp.int32)[:, None] < width[None, :]
    padded_kernel = jnp.pad(conv_weight, ((0, 1), (0, 0), (0, 0)))
    kernel = jnp.where(tap_mask[:, None, :], padded_kernel, jnp.zeros_like(padded_kernel))
    kernel = kernel.reshape((taps + 1) * embed_width, local_filters)
    valid = jnp.arange(length, dtype=jnp.int32)[:, None] + width[None, :] <= length
    letters = jnp.arange(alphabet, dtype=jnp.int32)

    def encode_block(block_chars):
        one_hot = (block_chars[:, :, None] == letters).astype(jnp.bfloat16)
        vectors = jnp.einsum(
            "bcn,ne->bce", one_hot, char_table, preferred_element_type=jnp.float32
        ).astype(jnp.bfloat16)
        shifted = jnp.pad(vectors, ((0, 0), (0, taps), (0, 0)))
        windows = jnp.concatenate(
            [shifted[:, tap : tap + length, :] for tap in range(taps + 1)], axis=2
        )
        conv = jnp.einsum("bpk,kf->bpf", windows, kernel, preferred_element_type=jnp.float32)
        conv = jnp.where(valid[None], conv, -jnp.inf)
        return jnp.maximum(jnp.max(conv, axis=1) + conv_bias, 0.0).astype(jnp.bfloat16)

    word_chars = chars[owner_types]
    block = math.gcd(unique_rows, 128)
    features = lax.map(encode_block, word_chars.reshape(unique_rows // block, block, length))
    features = features.reshape(unique_rows, local_filters)
    asked = lax.all_to_all(requests[0], "dp", split_axis=0, concat_axis=0, tiled=True)
    layer_input = features
    saved = []
    for layer in range(layers):
        weight_rows = hw_weight[layer].reshape(total_filters, 2 * local_filters)
        whole = lax.all_gather(layer_input, "enc", axis=1, tiled=True)
        pre = jnp.dot(whole, weight_rows, preferred_element_type=jnp.float32)
        transform = pre[:, :local_filters] + hw_bias[layer, 0]
        gate = jax.nn.sigmoid(pre[:, local_filters:] + hw_bias[layer, 1])
        saved.append((layer_input, whole, transform, gate))
        mixed = gate * jax.nn.silu(transform) + (1.0 - gate) * layer_input.astype(jnp.float32)
        layer_input = mixed.astype(jnp.bfloat16)
    partial_value = jnp.dot(layer_input, proj_weight, preferred_element_type=jnp.float32)
    encoded = (
        lax.psum_scatter(
            partial_value.astype(jnp.bfloat16), "enc", scatter_dimension=1, tiled=True
        ).astype(jnp.float32)
        + proj_bias
    ).astype(jnp.bfloat16)
    outgoing = encoded[jnp.maximum(asked, 0).reshape(-1)]
    returned = lax.all_to_all(outgoing, "dp", split_axis=0, concat_axis=0, tiled=True)
    token_vectors = returned[tok_slot]
    slot_total = returned.shape[0]
    slot_grads = jax.ops.segment_sum(
        d_tokens.astype(jnp.float32), tok_slot, num_segments=slot_total
    )
    arrived = lax.all_to_all(
        slot_grads.astype(jnp.bfloat16), "dp", split_axis=0, concat_axis=0, tiled=True
    )
    targets = jnp.where(asked >= 0, asked, unique_rows).reshape(-1)
    row_grads = jax.ops.segment_sum(
        arrived.astype(jnp.float32), targets, num_segments=unique_rows + 1
    )[:unique_rows]
    full_grads = lax.all_gather(row_grads.astype(jnp.bfloat16), "enc", axis=1, tiled=True)
    projection_term = lax.dot_general(
        layer_input, full_grads, (((0,), (0,)), ((), ())), preferred_element_type=jnp.float32
    )
    d_projection = lax.psum_scatter(
        projection_term.astype(jnp.bfloat16), "dp", scatter_dimension=1, tiled=True
    ).astype(jnp.float32)
    upstream = lax.dot_general(
        full_grads, proj_weight, (((1,), (1,)), ((), ())), preferred_element_type=jnp.float32
    )
    grads_by_layer = [None] * layers
    for layer in reversed(range(layers)):
        layer_in, whole, transform, gate = saved[layer]
        weight_rows = hw_weight[layer].reshape(total_filters, 2 * local_filters)
        sigma = jax.nn.sigmoid(transform)
        activated = transform * sigma
        slope = sigma * (1.0 + transform * (1.0 - sigma))
        transform_grad = upstream * gate * slope
        gate_grad = upstream * (activated - layer_in.astype(jnp.float32)) * gate * (1.0 - gate)
        pre_grads = jnp.concatenate([transform_grad, gate_grad], axis=1).astype(jnp.bfloat16)
        back_term = lax.dot_general(
            pre_grads, weight_rows, (((1,), (1,)), ((), ())), preferred_element_type=jnp.float32
        )
        upstream_next = upstream * (1.0 - gate) + lax.psum_scatter(
            back_term.astype(jnp.bfloat16), "enc", scatter_dimension=1, tiled=True
        ).astype(jnp.float32)
        weight_term = lax.psum_scatter(
            lax.dot_general(
                whole, pre_grads, (((0,), (0,)), ((), ())), preferred_element_type=jnp.float32
            ).astype(jnp.bfloat16),
            "dp",
            scatter_dimension=0,
            tiled=True,
        ).astype(jnp.float32)
        grads_by_layer[layer] = weight_term.reshape(weight_term.shape[0], 2, local_filters)
        upstream = upstream_next
    d_features = upstream.astype(jnp.bfloat16)
    d_highway = jnp.stack(grads_by_layer)
    return (token_vectors, d_features, d_highway, d_projection)


def solution(mesh):
    return jax.shard_map(
        per_device,
        mesh=mesh,
        in_specs=(
            P("dp", None),
            P(),
            P(None, None, "enc"),
            P("enc"),
            P(None, None, None, "enc"),
            P(None, None, "enc"),
            P("enc", None),
            P("enc"),
            P("dp"),
            P("dp", None, None),
            P("dp"),
            P("dp", "enc"),
        ),
        out_specs=(P("dp", "enc"), P("dp", "enc"), P(None, "dp", None, "enc"), P("enc", "dp")),
        check_vma=False,
    )
```

profile of v0, /device:TPU:1, one launch (start us, length us, event | category | flops | bytes accessed | tf_op | source)
XLA Modules:
  0.0 590.1 jit_solution(8828290828094214088)
XLA Ops:
  7.3 17.3 %copy.49 = s32[49152,50]{1,0:T(8,128)} copy(s32[49152,50]{0,1:T(8,128)} %param.14) | data formatting | bytes 19660800 | tf_op args[0]
  24.6 11.0 %gather_fusion = s32[1024,50]{1,0:T(8,128)S(1)} fusion(s32[49152,50]{1,0:T(8,128)} %copy.49, s32[1024]{0:T(1024)S(1)} %fusion.39), kind=kCustom, calls=%fused_computation | custom fusion | bytes 413696 | tf_op jit(solution)/shard_map/gather | solution.py:60
  35.9 20.9 %while.13 = (s32[]{:T(128)}, bf16[8,128,256]{2,1,0:T(8,128)(2,1)S(1)}, s32[8,128,50]{1,2,0:T(8,128)S(1)}, bf16[262,16]{0,1:T(8,128)(2,1)S(1)}, bf16[128,256]{1,0...) while((s32[]{:T(128)}, bf16[8,128,256]{2,1,0:T(8,128)(2,1)S(1)}, ...), condition=%wide.region_2.3_spmd.clone, body=%wide.region_0.2_spmd.clone.sunk | while | flops 478235136 | bytes 5421341 | solution.py:62
  57.9 5.7 fusion.50
  65.3 28.4 %all-gather.4.cloned.1.call-done = bf16[1024,2048]{0,1:T(8,128)(2,1)} async-done(((bf16[1024,256]{0,1:T(8,128)(2,1)}), bf16[1024,2048]{0,1:T(8,128)(2,1)}) %all-gather.4.cloned.1.call-update) | async-done | bytes 4194320 | tf_op jit(solution)/shard_map/all_gather | solution.py:69
  93.8 5.3 fusion.52
  101.2 6.7 %all-to-all-start = ((s32[16,1,256]{2,1,0:T(1,128)}), s32[16,1,256]{2,1,0:T(1,128)S(1)}, u32[]{:S(2)}, u32[]{:S(2)}) async-start(s32[16,1,256]{2,1,0:T(1,128)} %all_to_all.22), calls=%async_computation.1 | async-start | bytes 32768 | tf_op jit(solution)/shard_map/all_to_all | solution.py:64
  111.3 45.7 %scatter_custom_fusion = f32[4096,64]{1,0:T(8,128)} fusion(s32[8192]{0:T(1024)S(1)} %copy-done.8, f32[8192,64]{1,0:T(8,128)} %copy.55, f32[]{:T(128)} %constant.77.clone.1), kind=kCustom, calls=%fused_computation.68 | custom fusion | flops 524288 | bytes 1049088 | tf_op jit(solution)/shard_map/scatter-add | solution.py:87
  162.1 6.7 %all-to-all-start.2 = ((bf16[16,256,64]{1,2,0:T(8,128)(2,1)}), bf16[16,256,64]{1,2,0:T(8,128)(2,1)S(1)}, u32[]{:S(2)}, u32[]{:S(2)}) async-start(bf16[16,256,64]{1,2,0:T(8,128)(2,1)} %copy.56), calls=%async_computation.3 | async-start | bytes 1048576 | tf_op jit(solution)/shard_map/all_to_all | solution.py:90
  169.0 10.2 %all-to-all-done.2 = bf16[16,256,64]{1,2,0:T(8,128)(2,1)S(1)} async-done(((bf16[16,256,64]{1,2,0:T(8,128)(2,1)}), bf16[16,256,64]{1,2,0:T(8,128)(2,1)S(1)}, u32[]{:S(2)}, u32[]{:S(2)}) %all-to-all-start.2) | async-done | bytes 524320 | tf_op jit(solution)/shard_map/all_to_all | solution.py:90
  180.9 27.4 %scatter_custom_fusion.1 = f32[1025,64]{1,0:T(8,128)S(1)} fusion(s32[4096]{0:T(1024)S(1)} %bitcast.82, f32[4096,64]{1,0:T(8,128)} %bitcast.68, f32[]{:T(128)} %constant.77.clone.1), kind=kCustom, calls=%fused_computation.75 | custom fusion | flops 262144 | bytes 262912 | tf_op jit(solution)/shard_map/scatter-add | solution.py:94
  214.2 6.6 %fusion.53 = f32[1024,512]{0,1:T(8,128)} fusion(bf16[1024,2048]{0,1:T(8,128)(2,1)} %all-gather.6.cloned.1.call-done, bf16[2048,512]{1,0:T(8,128)(2,1)} %bitcast.71), kind=kOutput, calls=%fused_computation.107 | convolution fusion | flops 2147483648 | bytes 8388608 | tf_op jit(solution)/shard_map/dot_general | solution.py:70
  220.8 11.0 %all-gather.8.cloned.1.call-done = bf16[1024,512]{0,1:T(8,128)(2,1)} async-done(((bf16[1024,64]{0,1:T(8,128)(2,1)}), bf16[1024,512]{0,1:T(8,128)(2,1)}) %all-gather.8.cloned.1.call-update) | async-done | bytes 1048592 | tf_op jit(solution)/shard_map/all_gather | solution.py:97
  245.6 6.2 %convolution_convert_fusion.2 = bf16[2048,512]{1,0:T(8,128)(2,1)} fusion(bf16[1024,2048]{0,1:T(8,128)(2,1)} %all-gather.6.cloned.1.call-done, bf16[1024,256]{0,1:T(8,128)(2,1)} %copy-done.17, bf16[1024,256]{0,1:T(8,128)(2,1)} %copy-done.16), kind=kOutput, calls=%fused_computation.30 | convolution fusion | flops 2150629376 | bytes 7340032 | tf_op jit(solution)/shard_map/dot_general | solution.py:124
  252.0 23.9 %reduce-scatter.9.cloned.1.call-done = bf16[1024,256]{0,1:T(8,128)(2,1)} async-done(((bf16[1024,2048]{0,1:T(8,128)(2,1)}), bf16[1024,256]{0,1:T(8,128)(2,1)}) %reduce-scatter.9.cloned.1.call-update) | async-done | bytes 524304 | tf_op jit(solution)/shard_map/reduce_scatter | solution.py:120
  286.3 5.9 convolution_convert_fusion
  292.2 16.8 %reduce-scatter.7.cloned.1.call-done = bf16[1024,64]{0,1:T(8,128)(2,1)} async-done(((bf16[1024,512]{0,1:T(8,128)(2,1)}), bf16[1024,64]{0,1:T(8,128)(2,1)}) %reduce-scatter.7.cloned.1.call-update) | async-done | bytes 131088 | tf_op jit(solution)/shard_map/reduce_scatter | solution.py:78
  310.2 15.0 %gather_fusion.1 = bf16[4096,64]{1,0:T(8,128)(2,1)} fusion(bf16[1024,64]{1,0:T(8,128)(2,1)S(1)} %copy.52, s32[4096]{0:T(1024)S(1)} %broadcast_clamp_fusion), kind=kCustom, calls=%fused_computation.1 | custom fusion | bytes 1064960 | tf_op jit(solution)/shard_map/gather | solution.py:83
  327.6 6.9 %all-to-all-start.1 = ((bf16[16,256,64]{1,2,0:T(8,128)(2,1)}), bf16[16,256,64]{1,2,0:T(8,128)(2,1)}, u32[]{:S(2)}, u32[]{:S(2)}) async-start(bf16[16,256,64]{1,2,0:T(8,128)(2,1)} %copy.53), calls=%async_computation.2 | async-start | bytes 1048576 | tf_op jit(solution)/shard_map/all_to_all | solution.py:84
  334.5 52.2 %reduce-scatter.17.cloned.1.call-done = bf16[256,32]{0,1:T(8,128)(2,1)} async-done(((bf16[256,512]{0,1:T(8,128)(2,1)}), bf16[256,32]{0,1:T(8,128)(2,1)}) %reduce-scatter.17.cloned.1.call-update) | async-done | bytes 16400 | tf_op jit(solution)/shard_map/reduce_scatter | solution.py:101
  389.6 29.2 %gather_fusion.2 = bf16[8192,64]{1,0:T(8,128)(2,1)} fusion(bf16[4096,64]{1,0:T(8,128)(2,1)S(1)} %bitcast.63, s32[8192]{0:T(1024)S(1)} %fusion.38), kind=kCustom, calls=%fused_computation.2 | custom fusion | bytes 2129920 | tf_op jit(solution)/shard_map/gather | solution.py:85
  421.6 42.4 %reduce-scatter.15.cloned.1.call-done = bf16[128,512]{1,0:T(8,128)(2,1)} async-done(((bf16[2048,512]{1,0:T(8,128)(2,1)}), bf16[128,512]{1,0:T(8,128)(2,1)}) %reduce-scatter.15.cloned.1.call-update) | async-done | bytes 131088 | tf_op jit(solution)/shard_map/reduce_scatter | solution.py:123
  464.9 76.1 %reduce-scatter.13.cloned.1.call-done = bf16[128,512]{1,0:T(8,128)(2,1)} async-done(((bf16[2048,512]{1,0:T(8,128)(2,1)}), bf16[128,512]{1,0:T(8,128)(2,1)}) %reduce-scatter.13.cloned.1.call-update) | async-done | bytes 131088 | tf_op jit(solution)/shard_map/reduce_scatter | solution.py:123
  544.6 34.6 %reduce-scatter.11.cloned.1.call-done = bf16[1024,256]{0,1:T(8,128)(2,1)} async-done(((bf16[1024,2048]{0,1:T(8,128)(2,1)}), bf16[1024,256]{0,1:T(8,128)(2,1)}) %reduce-scatter.11.cloned.1.call-update) | async-done | bytes 524304 | tf_op jit(solution)/shard_map/reduce_scatter | solution.py:120
  (192 shorter events, 84.0 us)
Async XLA Ops:
  7.2 224.7 %copy-start = (bf16[256,512]{1,0:T(8,128)(2,1)S(1)}, bf16[256,512]{1,0:T(8,128)(2,1)}, u32[]{:S(2)}) copy-start(bf16[256,512]{1,0:T(8,128)(2,1)} %param.20) | copy-start | bytes 786436
  7.2 86.6 %all-gather.4.cloned.1.call-start = ((), (), s32[]{:S(2)}) async-start(), calls=%async_computation.9 | async-start | bytes 4718592 | tf_op jit(solution)/shard_map/all_gather | solution.py:69
  7.3 17.3 %copy-start.11 = (s32[1024]{0:T(1024)S(1)}, s32[1024]{0:T(1024)}, u32[]{:S(2)}) copy-start(s32[1024]{0:T(1024)} %param.22) | copy-start | bytes 12292
  24.6 11.2 %copy-start.7 = (bf16[7,16,256]{2,1,0:T(8,128)(2,1)S(1)}, bf16[7,16,256]{2,1,0:T(8,128)(2,1)}, u32[]{:S(2)}) copy-start(bf16[7,16,256]{2,1,0:T(8,128)(2,1)} %param.16) | copy-start | bytes 172036
  24.6 11.3 %copy-start.9 = (f32[256]{0:T(256)S(1)}, f32[256]{0:T(256)}, u32[]{:S(2)}) copy-start(f32[256]{0:T(256)} %param.17) | copy-start | bytes 3076
  24.6 11.3 %copy-start.15 = (bf16[262,16]{0,1:T(8,128)(2,1)S(1)}, bf16[262,16]{0,1:T(8,128)(2,1)}, u32[]{:S(2)}) copy-start(bf16[262,16]{0,1:T(8,128)(2,1)} %param.15) | copy-start | bytes 25156
  57.9 156.4 %all-gather.6.cloned.1.call-start = ((), (), s32[]{:S(2)}) async-start(), calls=%async_computation.10 | async-start | bytes 4718592 | tf_op jit(solution)/shard_map/all_gather | solution.py:69
  63.6 1.8 copy-start.12
  93.8 5.3 copy-start.3
  101.2 60.9 %all-to-all-start = ((s32[16,1,256]{2,1,0:T(1,128)}), s32[16,1,256]{2,1,0:T(1,128)S(1)}, u32[]{:S(2)}, u32[]{:S(2)}) async-start(s32[16,1,256]{2,1,0:T(1,128)} %all_to_all.22), calls=%async_computation.1 | async-start | bytes 32768 | tf_op jit(solution)/shard_map/all_to_all | solution.py:64
  107.9 3.4 copy-start.8
  162.1 17.1 %all-to-all-start.2 = ((bf16[16,256,64]{1,2,0:T(8,128)(2,1)}), bf16[16,256,64]{1,2,0:T(8,128)(2,1)S(1)}, u32[]{:S(2)}, u32[]{:S(2)}) async-start(bf16[16,256,64]{1,2,0:T(8,128)(2,1)} %copy.56), calls=%async_computation.3 | async-start | bytes 1048576 | tf_op jit(solution)/shard_map/all_to_all | solution.py:90
  168.7 63.1 %all-gather.8.cloned.1.call-start = ((), (), s32[]{:S(2)}) async-start(), calls=%async_computation.12 | async-start | bytes 1179648 | tf_op jit(solution)/shard_map/all_gather | solution.py:97
  210.8 65.1 %reduce-scatter.9.cloned.1.call-start = ((), (), s32[]{:S(2)}) async-start(), calls=%async_computation.13 | async-start | bytes 4718592 | tf_op jit(solution)/shard_map/reduce_scatter | solution.py:120
  231.8 5.3 copy-start.4
  241.5 67.6 %reduce-scatter.7.cloned.1.call-start = ((), (), s32[]{:S(2)}) async-start(), calls=%async_computation.11 | async-start | bytes 1179648 | tf_op jit(solution)/shard_map/reduce_scatter | solution.py:78
  243.0 143.7 %reduce-scatter.17.cloned.1.call-start = ((), (), s32[]{:S(2)}) async-start(), calls=%async_computation.17 | async-start | bytes 278528 | tf_op jit(solution)/shard_map/reduce_scatter | solution.py:101
  245.5 218.5 %reduce-scatter.15.cloned.1.call-start = ((), (), s32[]{:S(2)}) async-start(), calls=%async_computation.16 | async-start | bytes 2228224 | tf_op jit(solution)/shard_map/reduce_scatter | solution.py:123
  251.7 289.2 %reduce-scatter.13.cloned.1.call-start = ((), (), s32[]{:S(2)}) async-start(), calls=%async_computation.15 | async-start | bytes 2228224 | tf_op jit(solution)/shard_map/reduce_scatter | solution.py:123
  278.7 2.8 copy-start.14
  285.3 294.0 %reduce-scatter.11.cloned.1.call-start = ((), (), s32[]{:S(2)}) async-start(), calls=%async_computation.14 | async-start | bytes 4718592 | tf_op jit(solution)/shard_map/reduce_scatter | solution.py:120
  292.2 16.9 %copy-start.13 = (f32[64]{0:T(128)S(1)}, f32[64]{0:T(128)}, u32[]{:S(2)}) copy-start(f32[64]{0:T(128)} %param.21) | copy-start | bytes 772
  327.6 60.5 %all-to-all-start.1 = ((bf16[16,256,64]{1,2,0:T(8,128)(2,1)}), bf16[16,256,64]{1,2,0:T(8,128)(2,1)}, u32[]{:S(2)}, u32[]{:S(2)}) async-start(bf16[16,256,64]{1,2,0:T(8,128)(2,1)} %copy.53), calls=%async_computation.2 | async-start | bytes 1048576 | tf_op jit(solution)/shard_map/all_to_all | solution.py:84
  418.8 160.5 %copy-start.2 = (f32[1024,256]{0,1:T(8,128)S(1)}, f32[1024,256]{0,1:T(8,128)}, u32[]{:S(2)}) copy-start(f32[1024,256]{0,1:T(8,128)} %copy-done.1) | copy-start | bytes 3145732
  (6 other events, 6.1 us)
Sparse Core Ops, SparseCore 0:
  58.0 35.7 all-gather.3
  100.7 32.0 all-gather.5
  210.9 20.8 all-gather.7
  241.6 34.2 reduce-scatter.8
  278.1 30.8 reduce-scatter.6
  312.1 74.6 reduce-scatter.16
  390.3 73.6 reduce-scatter.14
  467.3 73.6 reduce-scatter.12
  543.5 35.6 reduce-scatter.10
where the time goes:
time: 594 us; the launch traced here: 590 us
  waiting for transfers between devices  296 us (50%)
  local copies, waits for them, and re-layouts  112 us (19%)
  other arithmetic  87.7 us (15%)
  matrix products  58.1 us (10%)
  starting transfers between devices  21 us (4%)
  between operations  14.1 us (2%)
    reduce_scatter x2, waiting for transfers between devices, per_device(): lax.psum_scatter(lax.dot_general(whole, pre_grads, (((0,), (0,)), ((), ()...  118 us
    reduce_scatter x2, waiting for transfers between devices, per_device(): lax.psum_scatter(back_term.astype(jnp.bfloat16), 'enc', scatter_dimension...  58.5 us
    reduce_scatter x1, waiting for transfers between devices, per_device(): lax.psum_scatter(projection_term.astype(jnp.bfloat16), 'dp', scatter_dime...  52.2 us
    scatter-add x1, other arithmetic, per_device(): jax.ops.segment_sum(d_tokens.astype(jnp.float32), tok_slot, num_segments=...  45.7 us
    unnamed x42, local copies, waits for them, and re-layouts  31.5 us
    gather x1, local copies, waits for them, and re-layouts, per_device(): token_vectors = returned[tok_slot]  29.2 us
    all_gather x2, waiting for transfers between devices, per_device(): whole = lax.all_gather(layer_input, 'enc', axis=1, tiled=True)  28.4 us
    scatter-add x1, other arithmetic, per_device(): jax.ops.segment_sum(arrived.astype(jnp.float32), targets, num_segments=un...  27.4 us
  transfers between devices with their start and end apart: 12, of which 9 were waited for; matrix products, arithmetic and copies ran while one was open for 31% of the time, Pallas kernels for 0%

commit v1 on v0

v1 whole, which is shorter than its diff:
```python
import functools
import jax
import jax.numpy as jnp
from jax import lax
from jax.experimental import pallas as pl
from jax.experimental.pallas import tpu as pltpu
from jax.sharding import PartitionSpec as P

BF = jnp.bfloat16
F32 = jnp.float32
VM = pl.BlockSpec(memory_space=pltpu.VMEM)
BASE = 128


def width_of(index, total):
    width = jnp.ones(index.shape, jnp.int32)
    for share in (1, 2, 4, 8, 16, 32):
        width = width + (index >= share * total // 64).astype(jnp.int32)
    return width


def one_hot(row, count):
    n = row.shape[1]
    return jnp.where(
        lax.broadcasted_iota(jnp.int32, (count, n), 0) == row, 1.0, 0.0
    ).astype(BF)


def nt(a, b):
    return lax.dot_general(a, b, (((1,), (1,)), ((), ())), preferred_element_type=F32)


def nn(a, b):
    return jnp.dot(a, b, preferred_element_type=F32)


def tn(a, b):
    return lax.dot_general(a, b, (((0,), (0,)), ((), ())), preferred_element_type=F32)


def column(row):
    return jnp.broadcast_to(row, (128, row.shape[1])).T[:, :1]


def encode_kernel(total, length, chars_ref, types_ref, table_ref, weight_ref, bias_ref,
                  out_ref, hot, lhs, acc, vec, band, best):
    step = pl.program_id(0)
    words = types_ref.shape[1]
    lanes = 256
    group = chars_ref.shape[1] // lanes
    rows = 64

    @pl.when(step == 0)
    def _():
        hot[...] = one_hot(types_ref[...] & (lanes - 1), lanes)
        acc[...] = jnp.zeros_like(acc)
        lhs[...] = jnp.zeros_like(lhs)

    high = types_ref[...] // lanes
    for part in range(group // 8):
        for j in range(8):
            block = chars_ref[:, (part * 8 + j) * lanes:(part * 8 + j + 1) * lanes]
            lhs[j * rows:j * rows + length, :] = (block - BASE).astype(F32).astype(BF)
        for half in range(words // 256):
            cols = slice(half * 256, half * 256 + 256)
            picked = nn(lhs[...], hot[:, cols])
            here = acc[:, cols]
            for j in range(8):
                here = jnp.where(high[:, cols] == step * group + part * 8 + j,
                                 picked[j * rows:(j + 1) * rows], here)
            acc[:, cols] = here

    @pl.when(step == pl.num_programs(0) - 1)
    def _():
        filters = weight_ref.shape[1]
        vec[length * 16:, :] = jnp.zeros((vec.shape[0] - length * 16, words), BF)

        def embed(p, carry):
            row = acc[pl.ds(p, 1), :].astype(jnp.int32) + BASE
            for b in range(words // 128):
                idx = jnp.broadcast_to(row[:, b * 128:(b + 1) * 128], (8, 128))
                low, seg = idx & 127, idx >> 7
                halves = []
                for h in range(2):
                    got = None
                    for s in range(3):
                        tab = table_ref[h * 8:(h + 1) * 8, s * 128:(s + 1) * 128]
                        val = jnp.take_along_axis(tab, low, axis=1)
                        got = val if got is None else jnp.where(seg == s, val, got)
                    halves.append(got)
                vec[pl.ds(pl.multiple_of(p * 16, 16), 16), b * 128:(b + 1) * 128] = (
                    jnp.concatenate(halves, axis=0).astype(BF))
            return carry

        lax.fori_loop(0, length, embed, 0)

        base = lax.axis_index("enc") * filters
        width_row = width_of(base + lax.broadcasted_iota(jnp.int32, (128, filters), 1), total)
        tap = lax.broadcasted_iota(jnp.int32, (128, filters), 0) // 16
        raw = jnp.concatenate(
            [weight_ref[...].astype(F32), jnp.zeros((128 - weight_ref.shape[0], filters), F32)],
            axis=0)
        kt = jnp.where(tap < width_row, raw, 0.0).T
        wide = jnp.concatenate([kt, jnp.zeros((filters, 128), F32)], axis=1)
        for q in range(8):
            moved = wide if q == 0 else pltpu.roll(wide, q * 16, 1)
            band[q * filters:(q + 1) * filters, :] = moved.astype(BF)
        best[...] = jnp.full(best.shape, -jnp.inf, F32)
        width_col = width_of(base + lax.broadcasted_iota(jnp.int32, (filters, 256), 0), total)
        groups = -(-length // 8)

        def conv(g, first, count, masked):
            for half in range(words // 256):
                cols = slice(half * 256, half * 256 + 256)
                win = vec[pl.ds(pl.multiple_of(g * 128, 128), 256), cols]
                out = nn(band[:count * filters, :], win)
                m = best[:, cols]
                for q in range(count):
                    val = out[q * filters:(q + 1) * filters]
                    if masked and first + q + 7 > length:
                        val = jnp.where(width_col <= length - first - q, val, -jnp.inf)
                    m = jnp.maximum(m, val)
                best[:, cols] = m

        def body(g, carry):
            conv(g, 0, 8, False)
            return carry

        lax.fori_loop(0, groups - 2, body, 0)
        for g in (groups - 2, groups - 1):
            conv(g, g * 8, min(8, length - g * 8), True)
        out_ref[...] = jnp.maximum(best[...] + column(bias_ref[...]), 0.0).astype(BF)


def encode(chars_t, types, table_t, weight, bias, total):
    length, count = chars_t.shape
    words = types.shape[1]
    filters = weight.shape[1]
    block = 4096
    return pl.pallas_call(
        functools.partial(encode_kernel, total, length),
        grid=(count // block,),
        in_specs=[pl.BlockSpec((length, block), lambda i: (0, i)), VM, VM, VM, VM],
        out_specs=VM,
        out_shape=jax.ShapeDtypeStruct((filters, words), BF),
        scratch_shapes=[
            pltpu.VMEM((256, words), BF),
            pltpu.VMEM((512, 256), BF),
            pltpu.VMEM((64, words), F32),
            pltpu.VMEM((1024, words), BF),
            pltpu.VMEM((8 * filters, 256), BF),
            pltpu.VMEM((filters, words), F32),
        ],
        compiler_params=pltpu.CompilerParams(vmem_limit_bytes=48 << 20),
    )(chars_t, types, table_t, weight, bias)


def slot_sums(slot_ref, d_ref, out_ref, acc, chunk=1024):
    c, tokens = d_ref.shape
    owners = out_ref.shape[0] // c
    acc[...] = jnp.zeros_like(acc)

    def body(i, carry):
        at = pl.ds(pl.multiple_of(i * chunk, chunk), chunk)
        slot = slot_ref[:, at]
        hot = one_hot(slot & 255, 256)
        high = slot >> 8
        d = d_ref[:, at]
        parts = [d * jnp.where(high == o, 1.0, 0.0).astype(BF) for o in range(owners)]
        acc[...] += nt(jnp.concatenate(parts, axis=0), hot)
        return carry

    lax.fori_loop(0, tokens // chunk, body, 0)
    out_ref[...] = acc[...].astype(BF)


def token_pick(slot_ref, ret_ref, out_ref, chunk=1024):
    c, tokens = out_ref.shape
    owners = ret_ref.shape[0] // c

    def body(i, carry):
        at = pl.ds(pl.multiple_of(i * chunk, chunk), chunk)
        slot = slot_ref[:, at]
        got = nn(ret_ref[...], one_hot(slot & 255, 256))
        high = slot >> 8
        out = jnp.zeros((c, chunk), F32)
        for o in range(owners):
            out = jnp.where(high == o, got[o * c:(o + 1) * c], out)
        out_ref[:, at] = out.astype(BF)
        return carry

    lax.fori_loop(0, tokens // chunk, body, 0)


def owner_sums(asked_ref, arr_ref, out_ref):
    c, unique = out_ref.shape
    reps, cap = asked_ref.shape
    acc = jnp.zeros((unique // 256 * c, 256), F32)
    for r in range(reps):
        asked = asked_ref[r:r + 1, :]
        hot = one_hot(asked & 255, 256)
        a = arr_ref[r * c:(r + 1) * c, :]
        parts = [a * jnp.where((asked >> 8) == h, 1.0, 0.0).astype(BF) for h in range(unique // 256)]
        acc += nt(jnp.concatenate(parts, axis=0), hot)
    for h in range(unique // 256):
        out_ref[:, h * 256:(h + 1) * 256] = acc[h * c:(h + 1) * c].astype(BF)


def owner_pick(asked_ref, enc_ref, out_ref):
    c, unique = enc_ref.shape
    reps, cap = asked_ref.shape
    enc = enc_ref[...]
    tall = jnp.concatenate([enc[:, h * 256:(h + 1) * 256] for h in range(unique // 256)], axis=0)
    for r in range(reps):
        asked = asked_ref[r:r + 1, :]
        got = nn(tall, one_hot(asked & 255, 256))
        out = jnp.zeros((c, cap), F32)
        for h in range(unique // 256):
            out = jnp.where((asked >> 8) == h, got[h * c:(h + 1) * c], out)
        out_ref[r * c:(r + 1) * c, :] = out.astype(BF)


def local(body, shape, scratch, *args):
    return pl.pallas_call(
        body, in_specs=[VM] * len(args), out_specs=VM,
        out_shape=jax.ShapeDtypeStruct(shape, BF), scratch_shapes=scratch,
        compiler_params=pltpu.CompilerParams(vmem_limit_bytes=48 << 20),
    )(*args)


def per_device(chars, char_table, conv_weight, conv_bias, hw_weight, hw_bias, proj_weight,
               proj_bias, owner_types, requests, tok_slot, d_tokens):
    taps, embed_width, filters = conv_weight.shape
    layers, total = hw_weight.shape[:2]
    unique = owner_types.shape[0]
    owners, cap = requests.shape[1:]
    tokens, c = d_tokens.shape
    table_t = jnp.pad(char_table.T.astype(F32), ((0, 0), (0, 384 - char_table.shape[0])))
    features = encode(chars.T, owner_types.reshape(1, unique), table_t,
                      conv_weight.reshape(taps * embed_width, filters),
                      conv_bias.reshape(1, filters), total)
    slot = tok_slot.reshape(1, tokens)
    asked = lax.all_to_all(requests[0], "dp", split_axis=0, concat_axis=0, tiled=True)
    slot_grads = local(slot_sums, (owners * c, cap), [pltpu.VMEM((owners * c, cap), F32)],
                       slot, d_tokens.T)
    arrived = lax.all_to_all(slot_grads, "dp", split_axis=0, concat_axis=0, tiled=True)
    row_grads = local(owner_sums, (c, unique), [], asked, arrived)
    full_grads = lax.all_gather(row_grads, "enc", axis=0, tiled=True)

    layer_input = features
    saved = []
    for layer in range(layers):
        rows = hw_weight[layer].reshape(total, 2 * filters)
        whole = lax.all_gather(layer_input, "enc", axis=0, tiled=True)
        pre = tn(rows, whole)
        transform = pre[:filters] + hw_bias[layer, 0][:, None]
        gate = jax.nn.sigmoid(pre[filters:] + hw_bias[layer, 1][:, None])
        saved.append((layer_input, whole, transform, gate))
        mixed = gate * jax.nn.silu(transform) + (1.0 - gate) * layer_input.astype(F32)
        layer_input = mixed.astype(BF)
    part = tn(proj_weight, layer_input)
    encoded = (lax.psum_scatter(part.astype(BF), "enc", scatter_dimension=0, tiled=True)
               .astype(F32) + proj_bias[:, None]).astype(BF)
    outgoing = local(owner_pick, (owners * c, cap), [], asked, encoded)
    returned = lax.all_to_all(outgoing, "dp", split_axis=0, concat_axis=0, tiled=True)
    token_vectors = local(token_pick, (c, tokens), [], slot, returned).T

    def scatter_dp(x):
        n = lax.axis_size("dp")
        got = lax.all_to_all(x.astype(BF), "dp", split_axis=0, concat_axis=0, tiled=True)
        return jnp.sum(got.reshape((n, got.shape[0] // n) + got.shape[1:]).astype(F32), axis=0)

    d_projection = scatter_dp(nt(full_grads, layer_input)).T
    upstream = nn(proj_weight, full_grads)
    grads = [None] * layers
    for layer in reversed(range(layers)):
        layer_in, whole, transform, gate = saved[layer]
        rows = hw_weight[layer].reshape(total, 2 * filters)
        sigma = jax.nn.sigmoid(transform)
        slope = sigma * (1.0 + transform * (1.0 - sigma))
        d_transform = upstream * gate * slope
        d_gate = upstream * (transform * sigma - layer_in.astype(F32)) * gate * (1.0 - gate)
        pre_grads = jnp.concatenate([d_transform, d_gate], axis=0).astype(BF)
        back = nn(rows, pre_grads).astype(BF)
        grads[layer] = scatter_dp(nt(whole, pre_grads)).reshape(-1, 2, filters)
        upstream = upstream * (1.0 - gate) + lax.psum_scatter(
            back, "enc", scatter_dimension=0, tiled=True).astype(F32)
    return token_vectors, upstream.T.astype(BF), jnp.stack(grads), d_projection


def solution(mesh):
    return jax.shard_map(
        per_device,
        mesh=mesh,
        in_specs=(
            P("dp", None), P(), P(None, None, "enc"), P("enc"), P(None, None, None, "enc"),
            P(None, None, "enc"), P("enc", None), P("enc"), P("dp"), P("dp", None, None),
            P("dp"), P("dp", "enc"),
        ),
        out_specs=(P("dp", "enc"), P("dp", "enc"), P(None, "dp", None, "enc"), P("enc", "dp")),
        check_vma=False,
    )
```

time: 594 us -> 319 us (0.54)
  the two profiles are of different devices: /device:TPU:1 before, /device:TPU:24 now
where the time goes in v1:
time: 319 us; the launch traced here: 318 us
  waiting for transfers between devices  144 us (45%)
  Pallas kernels  45.4 us (14%)
  matrix products  42.2 us (13%)
  starting transfers between devices  33.4 us (10%)
  local copies, waits for them, and re-layouts  20.1 us (6%)
  other arithmetic  17.9 us (6%)
  between operations  14.4 us (5%)
    all_to_all x3, waiting for transfers between devices, scatter_dp(): lax.all_to_all(x.astype(BF), 'dp', split_axis=0, concat_axis=0, tiled=True)  55.3 us
    reduce_scatter x2, waiting for transfers between devices, per_device(): lax.psum_scatter(back, 'enc', scatter_dimension=0, tiled=True).astype(F32)  33.4 us
    pallas_call x1, Pallas kernels, encode(): pl.pallas_call(functools.partial(encode_kernel, total, length), grid=(cou...  28.5 us
    all_gather x2, waiting for transfers between devices, per_device(): whole = lax.all_gather(layer_input, 'enc', axis=0, tiled=True)  25 us
    pallas_call x4, Pallas kernels, local(): pl.pallas_call(body, in_specs=[VM] * len(args), out_specs=VM, out_shape=j...  16.9 us
    all_to_all x3, starting transfers between devices, scatter_dp(): lax.all_to_all(x.astype(BF), 'dp', split_axis=0, concat_axis=0, tiled=True)  15.8 us
    dot_general x3, matrix products, nt(): lax.dot_general(a, b, (((1,), (1,)), ((), ())), preferred_element_type=F32)  14.8 us
    dot_general x3, matrix products, tn(): lax.dot_general(a, b, (((0,), (0,)), ((), ())), preferred_element_type=F32)  14.4 us
  transfers between devices with their start and end apart: 12, of which 9 were waited for; matrix products, arithmetic and copies ran while one was open for 17% of the time, Pallas kernels for 5%

profile of v1, /device:TPU:24, one launch (start us, length us, event | category | flops | bytes accessed | tf_op | source)
XLA Modules:
  0.0 317.9 jit_solution(7232461396877943412)
XLA Ops:
  10.2 28.5 %shard_map.147 = bf16[256,1024]{1,0:T(8,128)(2,1)} custom-call(s32[50,49152]{1,0:T(8,128)} %bitcast.67, s32[1,1024]{1,0:T(1,128)S(1)} %bitcast.65, f32[16,384]{1,0:T(8,128)S(1)} %pad_convert_fusion.table_ref, bf16[112,256]{1,0:T(8,128)(2,1)S(1)} %bitcast.64, f32[1,256]{1,0:T(1,128)S(1)} %bitcast.66), custom_call_target="tpu_custom_call" | custom-call | tf_op jit(solution)/shard_map/pallas_call | solution.py:140
  38.7 5.7 %fusion.28 = (bf16[1,2048,2,256]{3,2,1,0:T(2,128)(2,1)}, bf16[1,2048,2,256]{3,2,1,0:T(2,128)(2,1)S(1)}) fusion(bf16[2,2048,2,256]{3,2,1,0:T(2,128)(2,1)} %param.16), kind=kLoop, calls=%fused_computation.60 | loop fusion | bytes 8388608 | tf_op jit(solution)/shard_map/slice | solution.py:253
  46.2 25.0 %all-gather.4.cloned.1.call-done = bf16[2048,1024]{1,0:T(8,128)(2,1)} async-done(((bf16[256,1024]{1,0:T(8,128)(2,1)}), bf16[2048,1024]{1,0:T(8,128)(2,1)}) %all-gather.4.cloned.1.call-update) | async-done | bytes 4194320 | tf_op jit(solution)/shard_map/all_gather | solution.py:254
  71.2 5.2 %convolution_bitcast_fusion.1 = f32[512,1024]{1,0:T(8,128)S(1)} fusion(bf16[2048,1024]{1,0:T(8,128)(2,1)} %all-gather.4.cloned.1.call-done, bf16[2048,512]{1,0:T(8,128)(2,1)} %bitcast.70), kind=kOutput, calls=%fused_computation.7 | convolution fusion | flops 2147483648 | bytes 8388608 | tf_op jit(solution)/shard_map/dot_general | solution.py:38
  79.7 6.9 %all-to-all-start = ((s32[16,1,256]{2,1,0:T(1,128)}), s32[16,1,256]{2,1,0:T(1,128)S(1)}, u32[]{:S(2)}, u32[]{:S(2)}) async-start(s32[16,1,256]{2,1,0:T(1,128)} %all_to_all.39), calls=%async_computation | async-start | bytes 32768 | tf_op jit(solution)/shard_map/all_to_all | solution.py:243
  86.7 6.9 %shard_map.150 = bf16[1024,256]{1,0:T(8,128)(2,1)} custom-call(s32[1,8192]{1,0:T(1,128)S(1)} %bitcast.62, bf16[64,8192]{1,0:T(8,128)(2,1)S(1)} %bitcast.59), custom_call_target="tpu_custom_call" | custom-call | tf_op jit(solution)/shard_map/pallas_call | solution.py:224
  94.2 6.6 %all-to-all-start.2 = ((bf16[16,64,256]{2,1,0:T(8,128)(2,1)}), bf16[16,64,256]{2,1,0:T(8,128)(2,1)S(1)}, u32[]{:S(2)}, u32[]{:S(2)}) async-start(bf16[16,64,256]{2,1,0:T(8,128)(2,1)} %bitcast.17), calls=%async_computation.3 | async-start | bytes 1048576 | tf_op jit(solution)/shard_map/all_to_all | solution.py:246
  100.9 11.3 %all-to-all-done.2 = bf16[16,64,256]{2,1,0:T(8,128)(2,1)S(1)} async-done(((bf16[16,64,256]{2,1,0:T(8,128)(2,1)}), bf16[16,64,256]{2,1,0:T(8,128)(2,1)S(1)}, u32[]{:S(2)}, u32[]{:S(2)}) %all-to-all-start.2) | async-done | bytes 524320 | tf_op jit(solution)/shard_map/all_to_all | solution.py:246
  117.3 6.6 %convolution_bitcast_fusion = f32[512,1024]{1,0:T(8,128)} fusion(bf16[2048,1024]{1,0:T(8,128)(2,1)} %all-gather.6.cloned.1.call-done, bf16[2048,512]{1,0:T(8,128)(2,1)} %bitcast.74), kind=kOutput, calls=%fused_computation.6 | convolution fusion | flops 2147483648 | bytes 8388608 | tf_op jit(solution)/shard_map/dot_general | solution.py:38
  123.8 13.3 %all-gather.8.cloned.1.call-done = bf16[512,1024]{1,0:T(8,128)(2,1)} async-done(((bf16[64,1024]{1,0:T(8,128)(2,1)}), bf16[512,1024]{1,0:T(8,128)(2,1)}) %all-gather.8.cloned.1.call-update) | async-done | bytes 1048592 | tf_op jit(solution)/shard_map/all_gather | solution.py:248
  137.1 4.3 %multiply_convert_fusion.1 = (bf16[256,1024]{1,0:T(8,128)(2,1)S(1)}, bf16[256,1024]{1,0:T(8,128)(2,1)S(1)}, bf16[256,1024]{1,0:T(8,128)(2,1)}, f32[256,1024]{1,0:T(8,128)}) fusion(f32[512,1024]{1,0:T(8,128)} %convolution_bitcast_fusion, f32[256]{0:T(256)S(1)} %bitcast.88, f32[256]{0:T(256)S(1)} %bitcast.86, bf16[256,1024]{1,0:T(8,128)(2,1)S(1)} %copy-done.11, ...), kind=kOutput, calls=%fused_computation.45 | convolution fusion | flops 275513344 | bytes 6555648 | tf_op jit(solution)/shard_map/dot_general | solution.py:34
  142.3 4.3 %convert_bitcast_fusion.1 = bf16[2048,1024]{1,0:T(8,128)(2,1)} fusion(bf16[2048,512]{1,0:T(8,128)(2,1)S(1)} %bitcast.75, bf16[256,1024]{1,0:T(8,128)(2,1)S(1)} %get-tuple-element.17, bf16[256,1024]{1,0:T(8,128)(2,1)S(1)} %get-tuple-element.16), kind=kOutput, calls=%fused_computation.3 | convolution fusion | flops 2151677952 | bytes 7340032 | tf_op jit(solution)/shard_map/dot_general | solution.py:34
  149.3 33.4 %reduce-scatter.6.cloned.1.call-done = bf16[256,1024]{1,0:T(8,128)(2,1)} async-done(((bf16[2048,1024]{1,0:T(8,128)(2,1)}), bf16[256,1024]{1,0:T(8,128)(2,1)}) %reduce-scatter.6.cloned.1.call-update) | async-done | bytes 524304 | tf_op jit(solution)/shard_map/reduce_scatter | solution.py:286
  188.2 4.3 %convert_bitcast_fusion = bf16[2048,1024]{1,0:T(8,128)(2,1)} fusion(bf16[2048,512]{1,0:T(8,128)(2,1)S(1)} %bitcast.71, bf16[256,1024]{1,0:T(8,128)(2,1)S(1)} %fusion.6, bf16[256,1024]{1,0:T(8,128)(2,1)S(1)} %get-tuple-element.12), kind=kOutput, calls=%fused_computation.2 | convolution fusion | flops 2151677952 | bytes 7340032 | tf_op jit(solution)/shard_map/dot_general | solution.py:34
  196.0 6.8 %all-to-all-start.5 = ((bf16[16,32,256]{2,1,0:T(8,128)(2,1)}), bf16[16,32,256]{2,1,0:T(8,128)(2,1)S(1)}, u32[]{:S(2)}, u32[]{:S(2)}) async-start(bf16[16,32,256]{2,1,0:T(8,128)(2,1)} %bitcast.25), calls=%async_computation.8 | async-start | bytes 524288 | tf_op jit(solution)/shard_map/all_to_all | solution.py:270
  202.9 6.2 %convolution_convert_fusion = bf16[2048,512]{1,0:T(8,128)(2,1)} fusion(bf16[2048,1024]{1,0:T(8,128)(2,1)} %all-gather.6.cloned.1.call-done, bf16[256,1024]{1,0:T(8,128)(2,1)} %copy-done.20, bf16[256,1024]{1,0:T(8,128)(2,1)} %copy-done.19), kind=kOutput, calls=%fused_computation.4 | convolution fusion | flops 2150629376 | bytes 7340032 | tf_op jit(solution)/shard_map/dot_general | solution.py:30
  212.3 4.6 %all-to-all-start.4 = ((bf16[16,128,512]{2,1,0:T(8,128)(2,1)}), bf16[16,128,512]{2,1,0:T(8,128)(2,1)}, u32[]{:S(2)}, u32[]{:S(2)}) async-start(bf16[16,128,512]{2,1,0:T(8,128)(2,1)} %bitcast.72), calls=%async_computation.7 | async-start | bytes 4194304 | tf_op jit(solution)/shard_map/all_to_all | solution.py:270
  219.8 32.3 %all-to-all-done.4 = bf16[16,128,512]{2,1,0:T(8,128)(2,1)} async-done(((bf16[16,128,512]{2,1,0:T(8,128)(2,1)}), bf16[16,128,512]{2,1,0:T(8,128)(2,1)}, u32[]{:S(2)}, u32[]{:S(2)}) %all-to-all-start.4) | async-done | bytes 2097184 | tf_op jit(solution)/shard_map/all_to_all | solution.py:270
  252.1 3.6 %all-to-all-start.1 = ((bf16[16,64,256]{2,1,0:T(8,128)(2,1)}), bf16[16,64,256]{2,1,0:T(8,128)(2,1)S(1)}, u32[]{:S(2)}, u32[]{:S(2)}) async-start(bf16[16,64,256]{2,1,0:T(8,128)(2,1)} %bitcast.13), calls=%async_computation.2 | async-start | bytes 1048576 | tf_op jit(solution)/shard_map/all_to_all | solution.py:265
  255.6 6.2 %convolution_convert_fusion.1 = bf16[2048,512]{1,0:T(8,128)(2,1)} fusion(bf16[2048,1024]{1,0:T(8,128)(2,1)} %all-gather.4.cloned.1.call-done, bf16[256,1024]{1,0:T(8,128)(2,1)} %copy-done.15, bf16[256,1024]{1,0:T(8,128)(2,1)} %copy-done.13), kind=kOutput, calls=%fused_computation.5 | convolution fusion | flops 2150629376 | bytes 7340032 | tf_op jit(solution)/shard_map/dot_general | solution.py:30
  261.9 5.6 %all-to-all-done.1 = bf16[16,64,256]{2,1,0:T(8,128)(2,1)S(1)} async-done(((bf16[16,64,256]{2,1,0:T(8,128)(2,1)}), bf16[16,64,256]{2,1,0:T(8,128)(2,1)S(1)}, u32[]{:S(2)}, u32[]{:S(2)}) %all-to-all-start.1) | async-done | bytes 524320 | tf_op jit(solution)/shard_map/all_to_all | solution.py:265
  267.5 4.4 %all-to-all-start.3 = ((bf16[16,128,512]{2,1,0:T(8,128)(2,1)}), bf16[16,128,512]{2,1,0:T(8,128)(2,1)}, u32[]{:S(2)}, u32[]{:S(2)}) async-start(bf16[16,128,512]{2,1,0:T(8,128)(2,1)} %bitcast.73), calls=%async_computation.6 | async-start | bytes 4194304 | tf_op jit(solution)/shard_map/all_to_all | solution.py:270
  275.3 6.8 %shard_map.149 = bf16[64,8192]{1,0:T(8,128)(2,1)} custom-call(s32[1,8192]{1,0:T(1,128)S(1)} %bitcast.63, bf16[1024,256]{1,0:T(8,128)(2,1)S(1)} %bitcast.57), custom_call_target="tpu_custom_call" | custom-call | tf_op jit(solution)/shard_map/pallas_call | solution.py:224
  282.1 19.7 %all-to-all-done.3 = bf16[16,128,512]{2,1,0:T(8,128)(2,1)} async-done(((bf16[16,128,512]{2,1,0:T(8,128)(2,1)}), bf16[16,128,512]{2,1,0:T(8,128)(2,1)}, u32[]{:S(2)}, u32[]{:S(2)}) %all-to-all-start.3) | async-done | bytes 2097184 | tf_op jit(solution)/shard_map/all_to_all | solution.py:270
  (81 shorter events, 44.9 us)
Async XLA Ops:
  7.2 129.9 %copy-start = (bf16[256,512]{1,0:T(8,128)(2,1)S(1)}, bf16[256,512]{1,0:T(8,128)(2,1)}, u32[]{:S(2)}) copy-start(bf16[256,512]{1,0:T(8,128)(2,1)} %param.18) | copy-start | bytes 786436
  7.2 64.0 %all-gather.4.cloned.1.call-start = ((), (), s32[]{:S(2)}) async-start(), calls=%async_computation.9 | async-start | bytes 4718592 | tf_op jit(solution)/shard_map/all_gather | solution.py:254
  38.7 78.6 %all-gather.6.cloned.1.call-start = ((), (), s32[]{:S(2)}) async-start(), calls=%async_computation.10 | async-start | bytes 4718592 | tf_op jit(solution)/shard_map/all_gather | solution.py:254
  76.4 2.7 copy-start.16
  76.4 10.2 %copy-start.2 = (bf16[8192,64]{0,1:T(8,128)(2,1)S(1)}, bf16[8192,64]{0,1:T(8,128)(2,1)}, u32[]{:S(2)}) copy-start(bf16[8192,64]{0,1:T(8,128)(2,1)} %param.23) | copy-start | bytes 3145732
  76.4 10.2 %copy-start.3 = (s32[8192]{0:T(1024)S(1)}, s32[8192]{0:T(1024)}, u32[]{:S(2)}) copy-start(s32[8192]{0:T(1024)} %param.22) | copy-start | bytes 98308
  79.7 14.5 %all-to-all-start = ((s32[16,1,256]{2,1,0:T(1,128)}), s32[16,1,256]{2,1,0:T(1,128)S(1)}, u32[]{:S(2)}, u32[]{:S(2)}) async-start(s32[16,1,256]{2,1,0:T(1,128)} %all_to_all.39), calls=%async_computation | async-start | bytes 32768 | tf_op jit(solution)/shard_map/all_to_all | solution.py:243
  94.2 18.0 %all-to-all-start.2 = ((bf16[16,64,256]{2,1,0:T(8,128)(2,1)}), bf16[16,64,256]{2,1,0:T(8,128)(2,1)S(1)}, u32[]{:S(2)}, u32[]{:S(2)}) async-start(bf16[16,64,256]{2,1,0:T(8,128)(2,1)} %bitcast.17), calls=%async_computation.3 | async-start | bytes 1048576 | tf_op jit(solution)/shard_map/all_to_all | solution.py:246
  100.8 36.3 %all-gather.8.cloned.1.call-start = ((), (), s32[]{:S(2)}) async-start(), calls=%async_computation.12 | async-start | bytes 1179648 | tf_op jit(solution)/shard_map/all_gather | solution.py:248
  113.6 69.0 %reduce-scatter.6.cloned.1.call-start = ((), (), s32[]{:S(2)}) async-start(), calls=%async_computation.13 | async-start | bytes 4718592 | tf_op jit(solution)/shard_map/reduce_scatter | solution.py:286
  117.3 19.8 %copy-start.11 = (bf16[256,1024]{1,0:T(8,128)(2,1)S(1)}, bf16[256,1024]{1,0:T(8,128)(2,1)}, u32[]{:S(2)}) copy-start(bf16[256,1024]{1,0:T(8,128)(2,1)} %fusion.2) | copy-start | bytes 1572868
  137.1 5.1 %copy-start.10 = (bf16[256,8,2,256]{3,1,2,0:T(8,128)(2,1)S(1)}, bf16[256,8,2,256]{3,1,2,0:T(8,128)(2,1)}, u32[]{:S(2)}) copy-start(bf16[256,8,2,256]{3,1,2,0:T(8,128)(2,1)} %copy.29) | copy-start | bytes 6291460
  141.4 5.1 %copy-start.19 = (bf16[256,1024]{1,0:T(8,128)(2,1)}, bf16[256,1024]{1,0:T(8,128)(2,1)S(1)}, u32[]{:S(2)}) copy-start(bf16[256,1024]{1,0:T(8,128)(2,1)S(1)} %get-tuple-element.16) | copy-start | bytes 1572868
  146.6 36.1 %copy-start.12 = (f32[256,1024]{1,0:T(8,128)S(1)}, f32[256,1024]{1,0:T(8,128)}, u32[]{:S(2)}) copy-start(f32[256,1024]{1,0:T(8,128)} %get-tuple-element.23) | copy-start | bytes 3145732
  146.6 70.3 %reduce-scatter.4.cloned.1.call-start = ((), (), s32[]{:S(2)}) async-start(), calls=%async_computation.11 | async-start | bytes 1179648 | tf_op jit(solution)/shard_map/reduce_scatter | solution.py:262
  149.3 157.5 %reduce-scatter.8.cloned.1.call-start = ((), (), s32[]{:S(2)}) async-start(), calls=%async_computation.14 | async-start | bytes 4718592 | tf_op jit(solution)/shard_map/reduce_scatter | solution.py:286
  185.1 3.1 copy-start.9
  196.0 16.3 %all-to-all-start.5 = ((bf16[16,32,256]{2,1,0:T(8,128)(2,1)}), bf16[16,32,256]{2,1,0:T(8,128)(2,1)S(1)}, u32[]{:S(2)}, u32[]{:S(2)}) async-start(bf16[16,32,256]{2,1,0:T(8,128)(2,1)} %bitcast.25), calls=%async_computation.8 | async-start | bytes 524288 | tf_op jit(solution)/shard_map/all_to_all | solution.py:270
  212.3 4.6 %copy-start.18 = (f32[64]{0:T(128)S(1)}, f32[64]{0:T(128)}, u32[]{:S(2)}) copy-start(f32[64]{0:T(128)} %param.19) | copy-start | bytes 772
  212.3 39.7 %all-to-all-start.4 = ((bf16[16,128,512]{2,1,0:T(8,128)(2,1)}), bf16[16,128,512]{2,1,0:T(8,128)(2,1)}, u32[]{:S(2)}, u32[]{:S(2)}) async-start(bf16[16,128,512]{2,1,0:T(8,128)(2,1)} %bitcast.72), calls=%async_computation.7 | async-start | bytes 4194304 | tf_op jit(solution)/shard_map/all_to_all | solution.py:270
  252.1 15.4 %all-to-all-start.1 = ((bf16[16,64,256]{2,1,0:T(8,128)(2,1)}), bf16[16,64,256]{2,1,0:T(8,128)(2,1)S(1)}, u32[]{:S(2)}, u32[]{:S(2)}) async-start(bf16[16,64,256]{2,1,0:T(8,128)(2,1)} %bitcast.13), calls=%async_computation.2 | async-start | bytes 1048576 | tf_op jit(solution)/shard_map/all_to_all | solution.py:265
  267.5 34.4 %all-to-all-start.3 = ((bf16[16,128,512]{2,1,0:T(8,128)(2,1)}), bf16[16,128,512]{2,1,0:T(8,128)(2,1)}, u32[]{:S(2)}, u32[]{:S(2)}) async-start(bf16[16,128,512]{2,1,0:T(8,128)(2,1)} %bitcast.73), calls=%async_computation.6 | async-start | bytes 4194304 | tf_op jit(solution)/shard_map/all_to_all | solution.py:270
  282.1 24.6 %copy-start.8 = (f32[256,1024]{1,0:T(8,128)S(1)}, f32[256,1024]{1,0:T(8,128)}, u32[]{:S(2)}) copy-start(f32[256,1024]{1,0:T(8,128)} %copy-done.7) | copy-start | bytes 3145732
  304.6 6.4 %copy-start.1 = (bf16[256,512]{1,0:T(8,128)(2,1)S(1)}, bf16[256,512]{1,0:T(8,128)(2,1)}, u32[]{:S(2)}) copy-start(bf16[256,512]{1,0:T(8,128)(2,1)} %param.18) | copy-start | bytes 786436
  (9 other events, 11.3 us)
Sparse Core Ops, SparseCore 0:
  38.8 32.3 all-gather.3
  79.2 32.0 all-gather.5
  113.8 23.2 all-gather.7
  146.7 35.8 reduce-scatter.5
  184.9 31.2 reduce-scatter.3
  218.5 36.5 reduce-scatter.7

commit v2 on v1

--- a/solution.py
+++ b/solution.py
@@ -228,6 +228,486 @@
     )(*args)
 
 
+MESH = pl.DeviceIdType.MESH
+
+
+def send(src, dst, ssem, rsem, **to):
+    return pltpu.make_async_remote_copy(
+        src_ref=src, dst_ref=dst, send_sem=ssem, recv_sem=rsem, device_id=to, device_id_type=MESH)
+
+
+def rows_at(ref, start, count):
+    return ref.at[pl.ds(pl.multiple_of(start, count), count)]
+
+
+class Place:
+    def __init__(self):
+        e = lax.axis_index("enc")
+        self.chips = lax.axis_size("enc") // 2
+        self.y, self.k = e // 2, lax.rem(e, 2)
+        self.sib = self.y * 2 + 1 - self.k
+        self.right = self.at(1)
+        self.left = self.at(-1)
+
+    def at(self, d, other=False):
+        yy = lax.rem(self.y + d + self.chips, self.chips)
+        return yy * 2 + (1 - self.k if other else self.k)
+
+
+class Gather:
+    def __init__(self, place, whole, rows, ssem, rsem, index):
+        self.p, self.whole, self.rows = place, whole, rows
+        self.s = lambda i: ssem.at[index, i]
+        self.r = lambda i: rsem.at[index, i]
+
+    def half(self, e, which):
+        h = self.rows // 2
+        return rows_at(self.whole, e * self.rows + which * h, h)
+
+    def copy(self, i, ref, to):
+        return send(ref, ref, self.s(i), self.r(i), enc=to)
+
+    def start(self):
+        p = self.p
+        own = p.at(0)
+        self.sends = [
+            self.copy(0, self.half(own, 0), p.right),
+            self.copy(1, self.half(own, 1), p.left),
+            self.copy(2, self.half(own, 1), p.right),
+            self.copy(3, self.half(own, 0), p.left),
+            self.copy(4, rows_at(self.whole, own * self.rows, self.rows), p.sib),
+        ]
+        for c in self.sends:
+            c.start()
+
+    def more(self, i, ref, to):
+        c = self.copy(i, ref, to)
+        c.start()
+        self.sends.append(c)
+
+    def arrived(self, i, ref):
+        self.copy(i, ref, self.p.sib).wait_recv()
+
+    def forward1(self):
+        p = self.p
+        la, rb = self.half(p.at(-1), 0), self.half(p.at(1), 1)
+        self.arrived(0, la)
+        self.more(5, la, p.right)
+        self.arrived(1, rb)
+        self.more(6, rb, p.left)
+        self.more(7, la, p.sib)
+        self.more(8, rb, p.sib)
+
+    def forward2(self):
+        p = self.p
+        lb, ra = self.half(p.at(-1), 1), self.half(p.at(1), 0)
+        self.arrived(2, lb)
+        self.more(9, lb, p.sib)
+        self.arrived(3, ra)
+        self.more(10, ra, p.sib)
+
+    def wait_sib(self):
+        self.arrived(4, rows_at(self.whole, self.p.sib * self.rows, self.rows))
+
+    def forward3(self):
+        p = self.p
+        oa, ob = self.half(p.at(2), 0), self.half(p.at(2), 1)
+        self.arrived(5, oa)
+        self.more(11, oa, p.sib)
+        self.arrived(6, ob)
+        self.more(12, ob, p.sib)
+
+    def finish_near(self):
+        p = self.p
+        for i, d, h in ((7, -1, 0), (8, 1, 1), (9, -1, 1), (10, 1, 0)):
+            self.arrived(i, self.half(p.at(d, True), h))
+
+    def finish_far(self):
+        p = self.p
+        for i, h in ((11, 0), (12, 1)):
+            self.arrived(i, self.half(p.at(2, True), h))
+
+    def drain(self):
+        for c in self.sends:
+            c.wait_send()
+
+
+class Scatter:
+    def __init__(self, place, rows, bufs, ssem, rsem, index):
+        self.p, self.rows = place, rows
+        self.sib_out, self.sib_in, self.ring, self.xin, self.lin, self.rin, self.own = bufs
+        self.s = lambda i: ssem.at[index, i]
+        self.r = lambda i: rsem.at[index, i]
+        self.sends = []
+
+    def go(self, i, src, dst, to):
+        c = send(src, dst, self.s(i), self.r(i), enc=to)
+        c.start()
+        self.sends.append(c)
+
+    def arrived(self, i, dst):
+        send(dst, dst, self.s(i), self.r(i), enc=self.p.sib).wait_recv()
+
+    def block(self, ref, d, which=None):
+        if which is None:
+            return ref.at[d * self.rows:(d + 1) * self.rows]
+        h = self.rows // 2
+        return ref.at[d * self.rows + which * h:d * self.rows + (which + 1) * h]
+
+    def start(self, compute):
+        p = self.p
+        for d in (2, 1, 3, 0):
+            self.block(self.sib_out, d)[...] = compute(p.at(d, True)).astype(BF)
+            self.go(d, self.block(self.sib_out, d), self.block(self.sib_in, d), p.sib)
+        for d in (2, 1, 3, 0):
+            mine = compute(p.at(d))
+            other = self.block(self.sib_in, d)
+            self.arrived(d, other)
+            mine = mine + other[...].astype(F32)
+            if d == 0:
+                self.own[...] = mine
+                continue
+            self.block(self.ring, d)[...] = mine.astype(BF)
+            if d == 2:
+                self.go(4, self.block(self.ring, 2, 0), self.block(self.xin, 0, 0), p.right)
+                self.go(5, self.block(self.ring, 2, 1), self.block(self.xin, 0, 1), p.left)
+            if d == 1:
+                self.go(6, self.block(self.ring, 1, 1), self.block(self.lin, 0, 1), p.right)
+            if d == 3:
+                self.go(7, self.block(self.ring, 3, 0), self.block(self.rin, 0, 0), p.left)
+
+    def mid(self):
+        p = self.p
+        for i, d, h, dst, to in ((4, 1, 0, self.lin, p.right), (5, 3, 1, self.rin, p.left)):
+            came, mine = self.block(self.xin, 0, h), self.block(self.ring, d, h)
+            self.arrived(i, came)
+            mine[...] = (mine[...].astype(F32) + came[...].astype(F32)).astype(BF)
+            self.go(i + 4, mine, self.block(dst, 0, h), to)
+
+    def finish(self):
+        self.arrived(6, self.block(self.lin, 0, 1))
+        self.arrived(7, self.block(self.rin, 0, 0))
+        self.arrived(8, self.block(self.lin, 0, 0))
+        self.arrived(9, self.block(self.rin, 0, 1))
+
+    def drain(self):
+        for c in self.sends:
+            c.wait_send()
+
+
+def scatter_bufs(rows, n):
+    return [((4 * rows, n), BF)] * 3 + [((rows, n), BF)] * 3 + [((rows, n), F32)]
+
+
+class Exchange:
+    def __init__(self, src, dst, rows, ssem, rsem, index):
+        self.src, self.dst, self.rows = src, dst, rows
+        self.n = lax.axis_size("dp")
+        self.me = lax.axis_index("dp")
+        self.ssem, self.rsem, self.index = ssem, rsem, index
+
+    def at(self, ref, i):
+        return ref.at[i] if self.rows is None else rows_at(ref, i * self.rows, self.rows)
+
+    def copy(self, j):
+        to = lax.rem(self.me + j, self.n)
+        return send(self.at(self.src, to), self.at(self.dst, self.me),
+                    self.ssem.at[self.index, j], self.rsem.at[self.index, j], dp=to)
+
+    def start(self):
+        def body(j, carry):
+            self.copy(j).start()
+            return carry
+        lax.fori_loop(1, self.n, body, 0)
+        self.at(self.dst, self.me)[...] = self.at(self.src, self.me)[...]
+
+    def wait(self):
+        def body(j, carry):
+            came = self.at(self.dst, lax.rem(self.me - j + self.n, self.n))
+            send(came, came, self.ssem.at[self.index, j], self.rsem.at[self.index, j],
+                 dp=lax.rem(self.me + 1, self.n)).wait_recv()
+            return carry
+        lax.fori_loop(1, self.n, body, 0)
+
+    def drain(self):
+        def body(j, carry):
+            self.copy(j).wait_send()
+            return carry
+        lax.fori_loop(1, self.n, body, 0)
+
+
+def chunks(count, step, body):
+    def run(i, carry):
+        body(pl.ds(pl.multiple_of(i * step, step), step), i * step)
+        return carry
+    lax.fori_loop(0, count // step, run, 0)
+
+
+INPUTS = ("features", "weight", "bias", "proj", "pbias", "slot", "d_tokens", "requests")
+OUTPUTS = ("tokens", "d_features", "d_high", "d_proj")
+
+
+def step_kernel(names, *refs):
+    r = dict(zip(INPUTS + OUTPUTS + names, refs))
+    place = Place()
+    n_dp, me = lax.axis_size("dp"), lax.axis_index("dp")
+    filters, words = r["features"].shape
+    total = r["whole0"].shape[0]
+    c, tokens = r["d_tokens"].shape
+    cap = r["requests"].shape[2]
+    e = place.at(0)
+
+    barrier = pltpu.get_barrier_semaphore()
+    for to in (place.left, place.right, place.sib):
+        pl.semaphore_signal(barrier, inc=1, device_id={"enc": to}, device_id_type=MESH)
+
+    def greet(j, carry):
+        pl.semaphore_signal(barrier, inc=1, device_id={"dp": lax.rem(me + j, n_dp)},
+                            device_id_type=MESH)
+        return carry
+    lax.fori_loop(1, n_dp, greet, 0)
+
+    own_rows = pl.ds(pl.multiple_of(e * filters, filters), filters)
+    r["whole0"][own_rows, :] = r["features"][...]
+    pl.semaphore_wait(barrier, 3 + n_dp - 1)
+
+    gather = [Gather(place, r["whole0"], filters, r["ag_s"], r["ag_r"], 0),
+              Gather(place, r["whole1"], filters, r["ag_s"], r["ag_r"], 1),
+              Gather(place, r["grads"], c, r["ag_s"], r["ag_r"], 2)]
+    sums = [Scatter(place, filters, [r[f"rs{i}_{j}"] for j in range(7)], r["rs_s"], r["rs_r"], i)
+            for i in range(2)]
+    proj_sum = Scatter(place, c, [r[f"rs2_{j}"] for j in range(7)], r["rs_s"], r["rs_r"], 2)
+    high_rows = total // n_dp
+    proj_rows = r["proj"].shape[1] // n_dp
+
+    def exchange(src, dst, rows, index):
+        return Exchange(r[src], r[dst], rows, r["dp_s"], r["dp_r"], index)
+
+    asked = exchange("requests", "asked", None, 0)
+    slots = exchange("slot_out", "slot_in", c, 1)
+    picked = exchange("pick_out", "pick_in", c, 2)
+    d_proj = exchange("dp_out", "dp_in", proj_rows, 3)
+    d_high = [exchange("dh0_out", "dh0_in", high_rows, 4), exchange("dh1_out", "dh1_in", high_rows, 5)]
+
+    gather[0].start()
+    asked.start()
+
+    def layer(l, gat, whole, before, between, next_ref):
+        acc, weight = r["acc"], r["weight"]
+
+        def add(block, first=False):
+            at = pl.ds(pl.multiple_of(block * filters, filters), filters)
+            part = tn(weight[l, at, :], whole[at, :])
+            acc[...] = part if first else acc[...] + part
+
+        add(e, True)
+        before()
+        gat.forward1()
+        between()
+        gat.wait_sib()
+        add(place.sib)
+        gat.forward2()
+
+        def near(i, carry):
+            add(place.at(2 * i - 1))
+            return carry
+        lax.fori_loop(0, 2, near, 0)
+        gat.forward3()
+        add(place.at(2))
+        gat.finish_near()
+
+        def near_other(i, carry):
+            add(place.at(2 * i - 1, True))
+            return carry
+        lax.fori_loop(0, 2, near_other, 0)
+        gat.finish_far()
+        add(place.at(2, True))
+        bias = column(r["bias"][l:l + 1, :])
+        r["bcol"][...] = jnp.broadcast_to(bias, (2 * filters, 128))
+
+        def mix(at, start):
+            low = pl.ds(pl.multiple_of(filters + start, 32), 32)
+            t = acc[at, :] + jnp.tile(r["bcol"][at, :], (1, words // 128))
+            g = jax.nn.sigmoid(acc[low, :] + jnp.tile(r["bcol"][low, :], (1, words // 128)))
+            r["t"][l, at, :] = t
+            r["g"][l, at, :] = g
+            h = whole[pl.ds(pl.multiple_of(e * filters + start, 32), 32), :].astype(F32)
+            out = (g * (t * jax.nn.sigmoid(t)) + (1.0 - g) * h).astype(BF)
+            if next_ref is r["top"]:
+                next_ref[at, :] = out
+            else:
+                next_ref[pl.ds(pl.multiple_of(e * filters + start, 32), 32), :] = out
+        chunks(filters, 32, mix)
+        gat.drain()
+
+    n_chunks = tokens // 1024
+    r["sacc"][...] = jnp.zeros_like(r["sacc"])
+
+    def slot_part(first, last):
+        def body(i, carry):
+            at = pl.ds(pl.multiple_of(i * 1024, 1024), 1024)
+            slot = r["slot"][:, at]
+            hot = one_hot(slot & 255, 256)
+            high = slot >> 8
+            d = r["d_tokens"][:, at]
+            parts = [d * jnp.where(high == o, 1.0, 0.0).astype(BF) for o in range(n_dp)]
+            r["sacc"][...] += nt(jnp.concatenate(parts, axis=0), hot)
+            return carry
+        lax.fori_loop(first, last, body, 0)
+
+    def slot_rest():
+        slot_part(n_chunks // 2, n_chunks)
+        r["slot_out"][...] = r["sacc"][...].astype(BF)
+        slots.start()
+
+    layer(0, gather[0], r["whole0"], lambda: slot_part(0, n_chunks // 2), slot_rest, r["whole1"])
+    gather[1].start()
+    asked.wait()
+    for o in range(n_dp):
+        r["asked2"][o:o + 1, :] = r["asked"][o]
+
+    def owner_part():
+        slots.wait()
+        owner_sums(r["asked2"], r["slot_in"], r["row"])
+        r["grads"][pl.ds(pl.multiple_of(e * c, c), c), :] = r["row"][...]
+        gather[2].start()
+
+    layer(1, gather[1], r["whole1"], lambda: None, owner_part, r["top"])
+
+    top, proj = r["top"], r["proj"]
+    width = r["proj"].shape[1]
+    r["part"][...] = tn(proj[...], top[...])
+    proj_sum.start(lambda dest: r["part"][pl.ds(pl.multiple_of(dest * c, c), c), :])
+    gather[2].forward1()
+    gather[2].forward2()
+    gather[2].forward3()
+    gather[2].wait_sib()
+    gather[2].finish_near()
+    gather[2].finish_far()
+    up = r["up"]
+    up[...] = nn(proj[...], r["grads"][...])
+    proj_sum.mid()
+
+    def cell(l):
+        whole = r[f"whole{l}"]
+
+        def body(at, start):
+            t, g, u = r["t"][l, at, :], r["g"][l, at, :], up[at, :]
+            h = whole[pl.ds(pl.multiple_of(e * filters + start, 32), 32), :].astype(F32)
+            s = jax.nn.sigmoid(t)
+            r["pre"][l, at, :] = (u * g * (s * (1.0 + t * (1.0 - s)))).astype(BF)
+            low = pl.ds(pl.multiple_of(filters + start, 32), 32)
+            r["pre"][l, low, :] = (u * (t * s - h) * g * (1.0 - g)).astype(BF)
+            up[at, :] = u * (1.0 - g)
+        chunks(filters, 32, body)
+
+    def back(l):
+        return lambda dest: nn(
+            r["weight"][l, pl.ds(pl.multiple_of(dest * filters, filters), filters), :], r["pre"][l])
+
+    def high_term(l):
+        def body(at, start):
+            r[f"dh{l}_out"][at, :] = nt(r[f"whole{l}"][at, :], r["pre"][l]).astype(BF)
+        chunks(total, 256, body)
+        d_high[l].start()
+
+    def add_up(l, last):
+        s = sums[l]
+
+        def body(at, start):
+            new = up[at, :] + (s.own[at, :] + s.lin[at, :].astype(F32) + s.rin[at, :].astype(F32))
+            up[at, :] = new
+        chunks(filters, 32, body)
+
+    def high_sum(l):
+        def body(at, start):
+            got = jnp.zeros((32, 2 * filters), F32)
+            for i in range(n_dp):
+                got = got + r[f"dh{l}_in"][pl.ds(pl.multiple_of(i * high_rows + start, 32), 32), :].astype(F32)
+            r["d_high"][l, at, :] = got
+        d_high[l].wait()
+        chunks(high_rows, 32, body)
+
+    cell(1)
+    sums[1].start(back(1))
+    proj_sum.finish()
+    r["encoded"][...] = (
+        proj_sum.own[...] + proj_sum.lin[...].astype(F32) + proj_sum.rin[...].astype(F32)
+        + column(r["pbias"][...])[:c]).astype(BF)
+    owner_pick(r["asked2"], r["encoded"], r["pick_out"])
+    picked.start()
+    high_term(1)
+    sums[1].mid()
+    r["dp_out"][...] = nt(r["grads"][...], top[...]).astype(BF)
+    d_proj.start()
+    picked.wait()
+    token_pick(r["slot"], r["pick_in"], r["tokens"])
+    sums[1].finish()
+    add_up(1, False)
+    cell(0)
+    high_term(0)
+    sums[0].start(back(0))
+    d_proj.wait()
+    got = jnp.zeros((proj_rows, filters), F32)
+    for i in range(n_dp):
+        got = got + r["dp_in"][i * proj_rows:(i + 1) * proj_rows, :].astype(F32)
+    r["d_proj"][...] = got
+    high_sum(1)
+    sums[0].mid()
+    sums[0].finish()
+    add_up(0, True)
+    r["d_features"][...] = up[...].T.astype(BF)
+    high_sum(0)
+    for x in (asked, slots, picked, d_proj, d_high[0], d_high[1], gather[2], sums[0], sums[1], proj_sum):
+        x.drain()
+
+
+def step(features, weight, bias, proj, pbias, slot, d_tokens, requests, n_dp):
+    filters, words = features.shape
+    total = weight.shape[1]
+    c, tokens = d_tokens.shape
+    width = proj.shape[1]
+    cap = requests.shape[2]
+    bufs = {
+        "whole0": ((total, words), BF), "whole1": ((total, words), BF), "grads": ((width, words), BF),
+        "top": ((filters, words), BF), "acc": ((2 * filters, words), F32),
+        "bcol": ((2 * filters, 128), F32),
+        "t": ((2, filters, words), F32), "g": ((2, filters, words), F32),
+        "pre": ((2, 2 * filters, words), BF), "up": ((filters, words), F32),
+        "part": ((width, words), F32), "sacc": ((n_dp * c, cap), F32),
+        "slot_out": ((n_dp * c, cap), BF), "slot_in": ((n_dp * c, cap), BF),
+        "pick_out": ((n_dp * c, cap), BF), "pick_in": ((n_dp * c, cap), BF),
+        "row": ((c, words), BF), "encoded": ((c, words), BF),
+        "dp_out": ((width, filters), BF), "dp_in": ((width, filters), BF),
+        "asked": ((n_dp, 1, cap), jnp.int32), "asked2": ((n_dp, cap), jnp.int32),
+    }
+    for l in range(2):
+        for side in ("out", "in"):
+            bufs[f"dh{l}_{side}"] = ((total, 2 * filters), BF)
+    for i, rows in enumerate((filters, filters, c)):
+        for j, spec in enumerate(scatter_bufs(rows, words)):
+            bufs[f"rs{i}_{j}"] = spec
+    scratch = [pltpu.VMEM(*spec) for spec in bufs.values()]
+    sems = {"ag": (3, 13), "rs": (3, 10), "dp": (6, n_dp)}
+    names = tuple(bufs)
+    for name, dims in sems.items():
+        names += (name + "_s", name + "_r")
+        scratch += [pltpu.SemaphoreType.DMA(dims)] * 2
+    return pl.pallas_call(
+        functools.partial(step_kernel, names),
+        in_specs=[VM] * len(INPUTS), out_specs=[VM] * len(OUTPUTS),
+        out_shape=[
+            jax.ShapeDtypeStruct((c, tokens), BF),
+            jax.ShapeDtypeStruct((words, filters), BF),
+            jax.ShapeDtypeStruct((2, total // n_dp, 2 * filters), F32),
+            jax.ShapeDtypeStruct((width // n_dp, filters), F32),
+        ],
+        scratch_shapes=scratch,
+        compiler_params=pltpu.CompilerParams(
+            collective_id=0, has_side_effects=True, vmem_limit_bytes=62 << 20),
+    )(features, weight, bias, proj, pbias, slot, d_tokens, requests)
+
+
 def per_device(chars, char_table, conv_weight, conv_bias, hw_weight, hw_bias, proj_weight,
                proj_bias, owner_types, requests, tok_slot, d_tokens):
     taps, embed_width, filters = conv_weight.shape
@@ -239,53 +719,12 @@
     features = encode(chars.T, owner_types.reshape(1, unique), table_t,
                       conv_weight.reshape(taps * embed_width, filters),
                       conv_bias.reshape(1, filters), total)
-    slot = tok_slot.reshape(1, tokens)
-    asked = lax.all_to_all(requests[0], "dp", split_axis=0, concat_axis=0, tiled=True)
-    slot_grads = local(slot_sums, (owners * c, cap), [pltpu.VMEM((owners * c, cap), F32)],
-                       slot, d_tokens.T)
-    arrived = lax.all_to_all(slot_grads, "dp", split_axis=0, concat_axis=0, tiled=True)
-    row_grads = local(owner_sums, (c, unique), [], asked, arrived)
-    full_grads = lax.all_gather(row_grads, "enc", axis=0, tiled=True)
-
-    layer_input = features
-    saved = []
-    for layer in range(layers):
-        rows = hw_weight[layer].reshape(total, 2 * filters)
-        whole = lax.all_gather(layer_input, "enc", axis=0, tiled=True)
-        pre = tn(rows, whole)
-        transform = pre[:filters] + hw_bias[layer, 0][:, None]
-        gate = jax.nn.sigmoid(pre[filters:] + hw_bias[layer, 1][:, None])
-        saved.append((layer_input, whole, transform, gate))
-        mixed = gate * jax.nn.silu(transform) + (1.0 - gate) * layer_input.astype(F32)
-        layer_input = mixed.astype(BF)
-    part = tn(proj_weight, layer_input)
-    encoded = (lax.psum_scatter(part.astype(BF), "enc", scatter_dimension=0, tiled=True)
-               .astype(F32) + proj_bias[:, None]).astype(BF)
-    outgoing = local(owner_pick, (owners * c, cap), [], asked, encoded)
-    returned = lax.all_to_all(outgoing, "dp", split_axis=0, concat_axis=0, tiled=True)
-    token_vectors = local(token_pick, (c, tokens), [], slot, returned).T
-
-    def scatter_dp(x):
-        n = lax.axis_size("dp")
-        got = lax.all_to_all(x.astype(BF), "dp", split_axis=0, concat_axis=0, tiled=True)
-        return jnp.sum(got.reshape((n, got.shape[0] // n) + got.shape[1:]).astype(F32), axis=0)
-
-    d_projection = scatter_dp(nt(full_grads, layer_input)).T
-    upstream = nn(proj_weight, full_grads)
-    grads = [None] * layers
-    for layer in reversed(range(layers)):
-        layer_in, whole, transform, gate = saved[layer]
-        rows = hw_weight[layer].reshape(total, 2 * filters)
-        sigma = jax.nn.sigmoid(transform)
-        slope = sigma * (1.0 + transform * (1.0 - sigma))
-        d_transform = upstream * gate * slope
-        d_gate = upstream * (transform * sigma - layer_in.astype(F32)) * gate * (1.0 - gate)
-        pre_grads = jnp.concatenate([d_transform, d_gate], axis=0).astype(BF)
-        back = nn(rows, pre_grads).astype(BF)
-        grads[layer] = scatter_dp(nt(whole, pre_grads)).reshape(-1, 2, filters)
-        upstream = upstream * (1.0 - gate) + lax.psum_scatter(
-            back, "enc", scatter_dimension=0, tiled=True).astype(F32)
-    return token_vectors, upstream.T.astype(BF), jnp.stack(grads), d_projection
+    tok, d_feat, d_high, d_proj = step(
+        features, hw_weight.reshape(layers, total, 2 * filters),
+        hw_bias.reshape(layers, 2 * filters), proj_weight,
+        jnp.pad(proj_bias.reshape(1, c), ((0, 0), (0, 128 - c))),
+        tok_slot.reshape(1, tokens), d_tokens.T, requests.reshape(owners, 1, cap), owners)
+    return tok.T, d_feat, d_high.reshape(layers, -1, 2, filters), d_proj.T
 
 
 def solution(mesh):

time: 319 us -> 194 us (0.61)
  the two profiles are of different devices: /device:TPU:24 before, /device:TPU:1 now
where the time goes in v2:
time: 194 us; the launch traced here: 193 us
  Pallas kernels  171 us (88%)
  local copies, waits for them, and re-layouts  21.2 us (11%)
    pallas_call x1, Pallas kernels, step(): pl.pallas_call(functools.partial(step_kernel, names), in_specs=[VM] * len...  143 us
    pallas_call x1, Pallas kernels, encode(): pl.pallas_call(functools.partial(encode_kernel, total, length), grid=(cou...  27.7 us
    unnamed x14, local copies, waits for them, and re-layouts  9 us
    reshape x1, local copies, waits for them, and re-layouts, per_device(): hw_weight.reshape(layers, total, 2 * filters)  7.58 us

profile of v2, /device:TPU:1, one launch (start us, length us, event | category | flops | bytes accessed | tf_op | source)
XLA Modules:
  0.0 193.4 jit_solution(886348414574666507)
XLA Ops:
  0.6 1.2 pad.12.refs_4_
  1.8 1.3 copy.16
  3.1 1.3 reshape.42.refs_7_
  4.4 0.7 pad_convert_fusion.table_ref
  5.1 0.0 copy-start.1
  5.1 0.8 copy-done.1
  5.9 0.0 copy-start.2
  5.9 0.7 copy-done.2
  6.6 0.0 copy-start.3
  6.6 0.7 copy-done.3
  7.3 27.7 %shard_map.147.refs_0_ = bf16[256,1024]{1,0:T(8,128)(2,1)S(1)} custom-call(s32[50,49152]{1,0:T(8,128)} %bitcast.15, s32[1,1024]{1,0:T(1,128)S(1)} %bitcast.13, f32[16,384]{1,0:T(8,128)S(1)} %pad_convert_fusion.table_ref, bf16[112,256]{1,0:T(8,128)(2,1)S(1)} %bitcast.12, f32[1,256]{1,0:T(1,128)S(1)} %bitcast.14), custom_call_target="tpu_custom_call" | custom-call | tf_op jit(solution)/shard_map/pallas_call | solution.py:140
  35.0 0.0 copy-start
  35.0 0.8 copy-done
  35.8 7.6 %reshape.38.refs_1_ = bf16[2,2048,512]{2,1,0:T(8,128)(2,1)} reshape(bf16[2,2048,2,256]{3,2,1,0:T(2,128)(2,1)} %param.16) | data formatting | bytes 8388608 | tf_op jit(solution)/shard_map/reshape | solution.py:723
  43.4 143.1 %shard_map.148 = (bf16[64,8192]{1,0:T(8,128)(2,1)}, bf16[1024,256]{1,0:T(8,128)(2,1)}, f32[2,128,512]{2,1,0:T(8,128)}, f32[32,256]{1,0:T(8,128)}) custom-call(bf16[256,1024]{1,0:T(8,128)(2,1)} %copy-done, bf16[2,2048,512]{2,1,0:T(8,128)(2,1)} %reshape.38.refs_1_, f32[2,512]{1,0:T(2,128)} %bitcast.20, bf16[256,512]{1,0:T(8,128)(2,1)} %refs_3_.1, ...), custom_call_target="tpu_custom_call" | custom-call | tf_op jit(solution)/shard_map/pallas_call | solution.py:696
  186.5 0.0 copy-start.4
  186.5 2.2 %reshape.43 = f32[2,128,2,256]{3,2,1,0:T(2,128)} reshape(f32[2,128,512]{2,1,0:T(8,128)} %get-tuple-element.10) | data formatting | bytes 1048576 | tf_op jit(solution)/shard_map/reshape | solution.py:727
  188.6 2.3 %copy.20 = bf16[8192,64]{0,1:T(8,128)(2,1)} copy(bf16[8192,64]{0,1:T(8,128)(2,1)} %bitcast.16) | data formatting | bytes 2097152
  190.9 1.9 copy.21
  192.8 0.0 copy-done.4
  192.8 0.6 copy.22
Async XLA Ops:
  5.1 0.8 copy-start.1
  5.9 0.7 copy-start.2
  6.6 0.7 copy-start.3
  35.0 0.8 copy-start
  186.5 6.3 %copy-start.4 = (f32[32,256]{1,0:T(8,128)S(1)}, f32[32,256]{1,0:T(8,128)}, u32[]{:S(2)}) copy-start(f32[32,256]{1,0:T(8,128)} %get-tuple-element.11) | copy-start | bytes 98308

commit v3 on v2

--- a/solution.py
+++ b/solution.py
@@ -42,8 +42,8 @@
     return jnp.broadcast_to(row, (128, row.shape[1])).T[:, :1]
 
 
-def encode_kernel(total, length, chars_ref, types_ref, table_ref, weight_ref, bias_ref,
-                  out_ref, hot, lhs, acc, vec, band, best):
+def encode_kernel(total, length, chars_ref, types_ref, letters_ref, weight_ref, bias_ref,
+                  out_ref, hot, lhs, acc, vec, band, best, table_ref):
     step = pl.program_id(0)
     words = types_ref.shape[1]
     lanes = 256
@@ -55,6 +55,8 @@
         hot[...] = one_hot(types_ref[...] & (lanes - 1), lanes)
         acc[...] = jnp.zeros_like(acc)
         lhs[...] = jnp.zeros_like(lhs)
+        table_ref[...] = jnp.zeros_like(table_ref)
+        table_ref[:, :letters_ref.shape[1]] = letters_ref[...].astype(F32)
 
     high = types_ref[...] // lanes
     for part in range(group // 8):
@@ -150,6 +152,7 @@
             pltpu.VMEM((1024, words), BF),
             pltpu.VMEM((8 * filters, 256), BF),
             pltpu.VMEM((filters, words), F32),
+            pltpu.VMEM((16, 384), F32),
         ],
         compiler_params=pltpu.CompilerParams(vmem_limit_bytes=48 << 20),
     )(chars_t, types, table_t, weight, bias)
@@ -443,7 +446,7 @@
     lax.fori_loop(0, count // step, run, 0)
 
 
-INPUTS = ("features", "weight", "bias", "proj", "pbias", "slot", "d_tokens", "requests")
+INPUTS = ("features", "weight_in", "bias", "proj", "pbias", "slot", "d_tokens", "requests")
 OUTPUTS = ("tokens", "d_features", "d_high", "d_proj")
 
 
@@ -454,8 +457,12 @@
     filters, words = r["features"].shape
     total = r["whole0"].shape[0]
     c, tokens = r["d_tokens"].shape
-    cap = r["requests"].shape[2]
+    cap = r["requests"].shape[1]
     e = place.at(0)
+    raw = pltpu.make_async_copy(r["weight_in"].at[0], r["raw"], r["raw_s"].at[0])
+    raw.start()
+    for o in range(n_dp):
+        r["wanted"][o] = r["requests"][o:o + 1, :]
 
     barrier = pltpu.get_barrier_semaphore()
     for to in (place.left, place.right, place.sib):
@@ -474,7 +481,7 @@
     gather = [Gather(place, r["whole0"], filters, r["ag_s"], r["ag_r"], 0),
               Gather(place, r["whole1"], filters, r["ag_s"], r["ag_r"], 1),
               Gather(place, r["grads"], c, r["ag_s"], r["ag_r"], 2)]
-    sums = [Scatter(place, filters, [r[f"rs{i}_{j}"] for j in range(7)], r["rs_s"], r["rs_r"], i)
+    sums = [Scatter(place, filters, [r[f"rs{0 if j in (0, 2) else i}_{j}"] for j in range(7)], r["rs_s"], r["rs_r"], i)
             for i in range(2)]
     proj_sum = Scatter(place, c, [r[f"rs2_{j}"] for j in range(7)], r["rs_s"], r["rs_r"], 2)
     high_rows = total // n_dp
@@ -483,7 +490,7 @@
     def exchange(src, dst, rows, index):
         return Exchange(r[src], r[dst], rows, r["dp_s"], r["dp_r"], index)
 
-    asked = exchange("requests", "asked", None, 0)
+    asked = exchange("wanted", "asked", None, 0)
     slots = exchange("slot_out", "slot_in", c, 1)
     picked = exchange("pick_out", "pick_in", c, 2)
     d_proj = exchange("dp_out", "dp_in", proj_rows, 3)
@@ -492,6 +499,17 @@
     gather[0].start()
     asked.start()
 
+    def unpack(l):
+        raw.wait()
+
+        def body(at, start):
+            r["weight"][l, at, :] = r["raw"][at].reshape(64, 2 * filters)
+        chunks(total, 64, body)
+
+    unpack(0)
+    raw = pltpu.make_async_copy(r["weight_in"].at[1], r["raw"], r["raw_s"].at[1])
+    raw.start()
+
     def layer(l, gat, whole, before, between, next_ref):
         acc, weight = r["acc"], r["weight"]
 
@@ -500,8 +518,11 @@
             part = tn(weight[l, at, :], whole[at, :])
             acc[...] = part if first else acc[...] + part
 
+        if l == 1:
+            unpack(1)
         add(e, True)
-        before()
+        if before is not None:
+            before()
         gat.forward1()
         between()
         gat.wait_sib()
@@ -522,8 +543,9 @@
         lax.fori_loop(0, 2, near_other, 0)
         gat.finish_far()
         add(place.at(2, True))
-        bias = column(r["bias"][l:l + 1, :])
-        r["bcol"][...] = jnp.broadcast_to(bias, (2 * filters, 128))
+        for i in range(2):
+            r["bcol"][i * filters:(i + 1) * filters, :] = jnp.broadcast_to(
+                r["bias"][l, i:i + 1, :], (128, filters)).T
 
         def mix(at, start):
             low = pl.ds(pl.multiple_of(filters + start, 32), 32)
@@ -572,12 +594,12 @@
         r["grads"][pl.ds(pl.multiple_of(e * c, c), c), :] = r["row"][...]
         gather[2].start()
 
-    layer(1, gather[1], r["whole1"], lambda: None, owner_part, r["top"])
+    layer(1, gather[1], r["whole1"], None, owner_part, r["top"])
 
     top, proj = r["top"], r["proj"]
     width = r["proj"].shape[1]
-    r["part"][...] = tn(proj[...], top[...])
-    proj_sum.start(lambda dest: r["part"][pl.ds(pl.multiple_of(dest * c, c), c), :])
+    r["acc"][...] = tn(proj[...], top[...])
+    proj_sum.start(lambda dest: r["acc"][pl.ds(pl.multiple_of(dest * c, c), c), :])
     gather[2].forward1()
     gather[2].forward2()
     gather[2].forward3()
@@ -624,7 +646,8 @@
             got = jnp.zeros((32, 2 * filters), F32)
             for i in range(n_dp):
                 got = got + r[f"dh{l}_in"][pl.ds(pl.multiple_of(i * high_rows + start, 32), 32), :].astype(F32)
-            r["d_high"][l, at, :] = got
+            r["d_high"][l, at, 0, :] = got[:, :filters]
+            r["d_high"][l, at, 1, :] = got[:, filters:]
         d_high[l].wait()
         chunks(high_rows, 32, body)
 
@@ -633,7 +656,7 @@
     proj_sum.finish()
     r["encoded"][...] = (
         proj_sum.own[...] + proj_sum.lin[...].astype(F32) + proj_sum.rin[...].astype(F32)
-        + column(r["pbias"][...])[:c]).astype(BF)
+        + column(jnp.concatenate([r["pbias"][...], jnp.zeros((1, 128 - c), F32)], axis=1))[:c]).astype(BF)
     owner_pick(r["asked2"], r["encoded"], r["pick_out"])
     picked.start()
     high_term(1)
@@ -646,6 +669,7 @@
     add_up(1, False)
     cell(0)
     high_term(0)
+    sums[1].drain()
     sums[0].start(back(0))
     d_proj.wait()
     got = jnp.zeros((proj_rows, filters), F32)
@@ -658,7 +682,7 @@
     add_up(0, True)
     r["d_features"][...] = up[...].T.astype(BF)
     high_sum(0)
-    for x in (asked, slots, picked, d_proj, d_high[0], d_high[1], gather[2], sums[0], sums[1], proj_sum):
+    for x in (asked, slots, picked, d_proj, d_high[0], d_high[1], gather[2], sums[0], proj_sum):
         x.drain()
 
 
@@ -667,45 +691,61 @@
     total = weight.shape[1]
     c, tokens = d_tokens.shape
     width = proj.shape[1]
-    cap = requests.shape[2]
+    cap = requests.shape[1]
     bufs = {
         "whole0": ((total, words), BF), "whole1": ((total, words), BF), "grads": ((width, words), BF),
         "top": ((filters, words), BF), "acc": ((2 * filters, words), F32),
         "bcol": ((2 * filters, 128), F32),
         "t": ((2, filters, words), F32), "g": ((2, filters, words), F32),
         "pre": ((2, 2 * filters, words), BF), "up": ((filters, words), F32),
-        "part": ((width, words), F32), "sacc": ((n_dp * c, cap), F32),
+        "sacc": ((n_dp * c, cap), F32),
         "slot_out": ((n_dp * c, cap), BF), "slot_in": ((n_dp * c, cap), BF),
         "pick_out": ((n_dp * c, cap), BF), "pick_in": ((n_dp * c, cap), BF),
         "row": ((c, words), BF), "encoded": ((c, words), BF),
         "dp_out": ((width, filters), BF), "dp_in": ((width, filters), BF),
-        "asked": ((n_dp, 1, cap), jnp.int32), "asked2": ((n_dp, cap), jnp.int32),
+        "weight": ((2, total, 2 * filters), BF), "raw": ((total, 2, filters), BF),
+        "wanted": ((n_dp, 1, cap), jnp.int32), "asked": ((n_dp, 1, cap), jnp.int32), "asked2": ((n_dp, cap), jnp.int32),
     }
     for l in range(2):
         for side in ("out", "in"):
             bufs[f"dh{l}_{side}"] = ((total, 2 * filters), BF)
     for i, rows in enumerate((filters, filters, c)):
         for j, spec in enumerate(scatter_bufs(rows, words)):
-            bufs[f"rs{i}_{j}"] = spec
+            if i != 1 or j not in (0, 2):
+                bufs[f"rs{i}_{j}"] = spec
     scratch = [pltpu.VMEM(*spec) for spec in bufs.values()]
-    sems = {"ag": (3, 13), "rs": (3, 10), "dp": (6, n_dp)}
+    sems = {"ag": (3, 13), "rs": (3, 10), "dp": (6, n_dp), "raw": (2,)}
     names = tuple(bufs)
     for name, dims in sems.items():
         names += (name + "_s", name + "_r")
         scratch += [pltpu.SemaphoreType.DMA(dims)] * 2
     return pl.pallas_call(
         functools.partial(step_kernel, names),
-        in_specs=[VM] * len(INPUTS), out_specs=[VM] * len(OUTPUTS),
+        in_specs=[pl.BlockSpec(memory_space=pl.ANY) if x == "weight_in" else VM for x in INPUTS], out_specs=[VM] * len(OUTPUTS),
         out_shape=[
             jax.ShapeDtypeStruct((c, tokens), BF),
             jax.ShapeDtypeStruct((words, filters), BF),
-            jax.ShapeDtypeStruct((2, total // n_dp, 2 * filters), F32),
+            jax.ShapeDtypeStruct((2, total // n_dp, 2, filters), F32),
             jax.ShapeDtypeStruct((width // n_dp, filters), F32),
         ],
         scratch_shapes=scratch,
         compiler_params=pltpu.CompilerParams(
             collective_id=0, has_side_effects=True, vmem_limit_bytes=62 << 20),
     )(features, weight, bias, proj, pbias, slot, d_tokens, requests)
+
+
+def hand_on(*arrays):
+    n = len(arrays)
+
+    def kernel(*refs):
+        for i in range(n):
+            refs[n + i][...] = refs[i][...]
+
+    return pl.pallas_call(
+        kernel, in_specs=[VM] * n, out_specs=[VM] * n,
+        out_shape=[jax.ShapeDtypeStruct(a.shape, a.dtype) for a in arrays],
+        compiler_params=pltpu.CompilerParams(vmem_limit_bytes=32 << 20),
+    )(*arrays)
 
 
 def per_device(chars, char_table, conv_weight, conv_bias, hw_weight, hw_bias, proj_weight,
@@ -715,16 +755,14 @@
     unique = owner_types.shape[0]
     owners, cap = requests.shape[1:]
     tokens, c = d_tokens.shape
-    table_t = jnp.pad(char_table.T.astype(F32), ((0, 0), (0, 384 - char_table.shape[0])))
-    features = encode(chars.T, owner_types.reshape(1, unique), table_t,
+    features = encode(chars.T, owner_types.reshape(1, unique), char_table.T,
                       conv_weight.reshape(taps * embed_width, filters),
                       conv_bias.reshape(1, filters), total)
-    tok, d_feat, d_high, d_proj = step(
-        features, hw_weight.reshape(layers, total, 2 * filters),
-        hw_bias.reshape(layers, 2 * filters), proj_weight,
-        jnp.pad(proj_bias.reshape(1, c), ((0, 0), (0, 128 - c))),
-        tok_slot.reshape(1, tokens), d_tokens.T, requests.reshape(owners, 1, cap), owners)
-    return tok.T, d_feat, d_high.reshape(layers, -1, 2, filters), d_proj.T
+    outs = step(
+        features, hw_weight, hw_bias, proj_weight, proj_bias.reshape(1, c),
+        tok_slot.reshape(1, tokens), d_tokens.T, requests.reshape(owners, cap), owners)
+    tok, d_feat, d_high, d_proj = hand_on(*outs)
+    return tok.T, d_feat, d_high, d_proj.T
 
 
 def solution(mesh):

time: 194 us -> 180 us (0.928)
  local copies, waits for them, and re-layouts: 21.2 us -> 7.73 us
    reshape x3 -> x0, local copies, waits for them, and re-layouts: 11.1 us -> none  [the longest x1 7.58 us: per_device(): hw_weight.reshape(layers, total, 2 * filters)]
    unnamed x14 -> x18, local copies, waits for them, and re-layouts: 9 us -> 7.73 us
    pallas_call x1 -> x2, Pallas kernels: 143 us -> 143 us  [the longest x1 142 us: step(): pl.pallas_call(functools.partial(step_kernel, names), in_specs=[pl.BlockS...]
where the time goes in v3:
time: 180 us
  Pallas kernels  171 us (95%)
  local copies, waits for them, and re-layouts  7.73 us (4%)
    pallas_call x1, Pallas kernels, step(): pl.pallas_call(functools.partial(step_kernel, names), in_specs=[pl.BlockS...  142 us
    pallas_call x1, Pallas kernels, encode(): pl.pallas_call(functools.partial(encode_kernel, total, length), grid=(cou...  27.7 us
    unnamed x18, local copies, waits for them, and re-layouts  7.73 us

profile of v3, /device:TPU:1, one launch (start us, length us, event | category | flops | bytes accessed | tf_op | source)
XLA Modules:
  0.0 179.5 jit_solution(5218922013181166168)
XLA Ops:
  0.6 0.0 copy-start.4
  0.6 0.8 copy-done.4
  1.5 0.0 copy-start.6
  1.5 0.7 copy-done.6
  2.2 0.0 copy-start.7
  2.2 0.7 copy-done.7
  2.8 0.0 copy-start.8
  2.8 0.7 copy-done.8
  3.5 27.7 %shard_map.147.refs_0_ = bf16[256,1024]{1,0:T(8,128)(2,1)S(1)} custom-call(s32[50,49152]{1,0:T(8,128)} %bitcast.15, s32[1,1024]{1,0:T(1,128)S(1)} %bitcast.13, bf16[16,262]{1,0:T(8,128)(2,1)S(1)} %bitcast.12, bf16[112,256]{1,0:T(8,128)(2,1)S(1)} %bitcast.11, f32[1,256]{1,0:T(1,128)S(1)} %bitcast.14), custom_call_target="tpu_custom_call" | custom-call | tf_op jit(solution)/shard_map/pallas_call | solution.py:142
  31.3 0.0 copy-start
  31.3 0.8 copy-done
  32.1 141.9 %shard_map.148 = (bf16[64,8192]{1,0:T(8,128)(2,1)}, bf16[1024,256]{1,0:T(8,128)(2,1)}, f32[2,128,2,256]{3,2,1,0:T(2,128)}, f32[32,256]{1,0:T(8,128)}) custom-call(bf16[256,1024]{1,0:T(8,128)(2,1)} %copy-done, bf16[2,2048,2,256]{3,2,1,0:T(2,128)(2,1)} %refs_1_.1, f32[2,2,256]{2,1,0:T(2,128)} %refs_2_.1, bf16[256,512]{1,0:T(8,128)(2,1)} %refs_3_.1, ...), custom_call_target="tpu_custom_call" | custom-call | tf_op jit(solution)/shard_map/pallas_call | solution.py:722
  174.0 0.0 copy-start.1
  174.0 1.2 copy-done.1
  175.2 0.0 copy-start.2
  175.2 1.0 copy-done.2
  176.3 0.0 copy-start.3
  176.3 1.0 copy-done.3
  177.3 0.0 copy-start.5
  177.3 0.8 copy-done.5
  178.1 1.4 shard_map.149
Async XLA Ops:
  0.6 0.8 copy-start.4
  1.5 0.7 copy-start.6
  2.2 0.7 copy-start.7
  2.8 0.7 copy-start.8
  31.3 0.8 copy-start
  174.0 1.2 copy-start.1
  175.2 1.0 copy-start.2
  176.3 1.0 copy-start.3
  177.3 0.8 copy-start.5

commit v4 on v3

--- a/solution.py
+++ b/solution.py
@@ -1,3 +1,4 @@
+import math
 import functools
 import jax
 import jax.numpy as jnp
@@ -154,7 +155,7 @@
             pltpu.VMEM((filters, words), F32),
             pltpu.VMEM((16, 384), F32),
         ],
-        compiler_params=pltpu.CompilerParams(vmem_limit_bytes=48 << 20),
+        compiler_params=pltpu.CompilerParams(vmem_limit_bytes=63 << 20),
     )(chars_t, types, table_t, weight, bias)
 
 
@@ -398,6 +399,121 @@
             c.wait_send()
 
 
+class Ring:
+    def __init__(self, block, half, bufs, plus, minus, ssem, rsem, index):
+        self.block, self.half, self.plus, self.minus = block, half, plus, minus
+        self.xin, self.lin, self.rin = bufs
+        self.s = lambda i: ssem.at[index, i]
+        self.r = lambda i: rsem.at[index, i]
+        self.sends = []
+
+    def go(self, i, src, dst, to):
+        c = send(src, dst, self.s(i), self.r(i), dp=to)
+        c.start()
+        self.sends.append(c)
+
+    def arrived(self, i, dst):
+        send(dst, dst, self.s(i), self.r(i), dp=self.plus).wait_recv()
+
+    def start(self):
+        self.go(0, self.block(2, 0), self.half(self.xin, 0), self.plus)
+        self.go(1, self.block(2, 1), self.half(self.xin, 1), self.minus)
+        self.go(2, self.block(1, 1), self.half(self.lin, 1), self.plus)
+        self.go(3, self.block(3, 0), self.half(self.rin, 0), self.minus)
+
+    def mid(self):
+        for i, d, h, dst, to in ((0, 1, 0, self.lin, self.plus), (1, 3, 1, self.rin, self.minus)):
+            came, mine = self.half(self.xin, h), self.block(d, h)
+            self.arrived(i, came)
+            mine[...] = (mine[...].astype(F32) + came[...].astype(F32)).astype(BF)
+            self.go(4 + i, mine, self.half(dst, h), to)
+
+    def finish(self):
+        self.arrived(2, self.half(self.lin, 1))
+        self.arrived(3, self.half(self.rin, 0))
+        self.arrived(4, self.half(self.lin, 0))
+        self.arrived(5, self.half(self.rin, 1))
+
+    def drain(self):
+        for c in self.sends:
+            c.wait_send()
+
+
+class Plane:
+    def __init__(self, out, bufs, ssem, rsem, index):
+        n = lax.axis_size("dp")
+        side = math.isqrt(n)
+        me = lax.axis_index("dp")
+        z, x = me // side, lax.rem(me, side)
+        self.out, self.z, self.x = out, z, x
+        rows, cols = out.shape[2], out.shape[3] // 2
+        self.cols = cols
+
+        def step_x(d):
+            return lax.rem(x + d, side)
+
+        def step_z(d):
+            return lax.rem(z + d, side)
+
+        along_x = (z * side + step_x(1), z * side + step_x(side - 1))
+        along_z = (step_z(1) * side + x, step_z(side - 1) * side + x)
+        two = lambda h: slice(2 * h, 2 * h + 2)
+        part = lambda h: slice(h * rows // 2, (h + 1) * rows // 2)
+        first, second, self.mids = bufs[0:6], bufs[6:12], bufs[12:14]
+        half1 = lambda ref, h: ref.at[two(h)]
+        half2 = lambda ref, h: ref.at[part(h)]
+        self.first = [
+            Ring(lambda d, h: out.at[two(h), step_x(d), :, :cols], half1, first[:3], *along_x,
+                 ssem, rsem, index),
+            Ring(lambda d, h: out.at[step_z(d), two(h), :, cols:], half1, first[3:], *along_z,
+                 ssem, rsem, index + 1),
+        ]
+        self.second = [
+            Ring(lambda d, h: self.mids[0].at[step_z(d), part(h)], half2, second[:3], *along_z,
+                 ssem, rsem, index + 2),
+            Ring(lambda d, h: self.mids[1].at[step_x(d), part(h)], half2, second[3:], *along_x,
+                 ssem, rsem, index + 3),
+        ]
+
+    def start(self):
+        for ring in self.first:
+            ring.start()
+
+    def mid(self):
+        for ring in self.first:
+            ring.mid()
+
+    def turn(self):
+        for i, ring in enumerate(self.first):
+            ring.finish()
+            own = (self.out[:, self.x, :, :self.cols] if i == 0
+                   else self.out[self.z, :, :, self.cols:])
+            self.mids[i][...] = (own.astype(F32) + ring.lin[...].astype(F32)
+                                 + ring.rin[...].astype(F32)).astype(BF)
+        for ring in self.second:
+            ring.start()
+
+    def mid2(self):
+        for ring in self.second:
+            ring.mid()
+
+    def finish(self):
+        got = []
+        for i, ring in enumerate(self.second):
+            ring.finish()
+            own = self.mids[i][self.z if i == 0 else self.x]
+            got.append(own.astype(F32) + ring.lin[...].astype(F32) + ring.rin[...].astype(F32))
+        return got
+
+    def drain(self):
+        for ring in self.first + self.second:
+            ring.drain()
+
+
+def plane_bufs(side, rows, cols):
+    return [((side, rows, cols), BF)] * 6 + [((rows, cols), BF)] * 6 + [((side, rows, cols), BF)] * 2
+
+
 def scatter_bufs(rows, n):
     return [((4 * rows, n), BF)] * 3 + [((rows, n), BF)] * 3 + [((rows, n), F32)]
 
@@ -494,7 +610,8 @@
     slots = exchange("slot_out", "slot_in", c, 1)
     picked = exchange("pick_out", "pick_in", c, 2)
     d_proj = exchange("dp_out", "dp_in", proj_rows, 3)
-    d_high = [exchange("dh0_out", "dh0_in", high_rows, 4), exchange("dh1_out", "dh1_in", high_rows, 5)]
+    d_high = [Plane(r[f"dh{l}_out"], [r[f"dh{l}_{j}"] for j in range(14)], r["ring_s"], r["ring_r"], 4 * l)
+              for l in range(2)]
 
     gather[0].start()
     asked.start()
@@ -628,9 +745,16 @@
             r["weight"][l, pl.ds(pl.multiple_of(dest * filters, filters), filters), :], r["pre"][l])
 
     def high_term(l):
-        def body(at, start):
-            r[f"dh{l}_out"][at, :] = nt(r[f"whole{l}"][at, :], r["pre"][l]).astype(BF)
-        chunks(total, 256, body)
+        out = r[f"dh{l}_out"]
+        side = out.shape[0]
+
+        def body(z, carry):
+            for x in range(0, side, 2):
+                at = pl.ds(pl.multiple_of((z * side + x) * high_rows, 2 * high_rows), 2 * high_rows)
+                got = nt(r[f"whole{l}"][at, :], r["pre"][l]).astype(BF)
+                out[z, x:x + 2] = got.reshape(2, high_rows, 2 * filters)
+            return carry
+        lax.fori_loop(0, side, body, 0)
         d_high[l].start()
 
     def add_up(l, last):
@@ -642,14 +766,8 @@
         chunks(filters, 32, body)
 
     def high_sum(l):
-        def body(at, start):
-            got = jnp.zeros((32, 2 * filters), F32)
-            for i in range(n_dp):
-                got = got + r[f"dh{l}_in"][pl.ds(pl.multiple_of(i * high_rows + start, 32), 32), :].astype(F32)
-            r["d_high"][l, at, 0, :] = got[:, :filters]
-            r["d_high"][l, at, 1, :] = got[:, filters:]
-        d_high[l].wait()
-        chunks(high_rows, 32, body)
+        for i, got in enumerate(d_high[l].finish()):
+            r["d_high"][l, :, i, :] = got
 
     cell(1)
     sums[1].start(back(1))
@@ -661,23 +779,29 @@
     picked.start()
     high_term(1)
     sums[1].mid()
+    d_high[1].mid()
     r["dp_out"][...] = nt(r["grads"][...], top[...]).astype(BF)
     d_proj.start()
-    picked.wait()
-    token_pick(r["slot"], r["pick_in"], r["tokens"])
+    d_high[1].turn()
     sums[1].finish()
     add_up(1, False)
     cell(0)
+    sums[1].drain()
     high_term(0)
-    sums[1].drain()
     sums[0].start(back(0))
+    d_high[1].mid2()
+    d_high[0].mid()
+    sums[0].mid()
+    picked.wait()
+    token_pick(r["slot"], r["pick_in"], r["tokens"])
+    high_sum(1)
+    d_high[0].turn()
     d_proj.wait()
     got = jnp.zeros((proj_rows, filters), F32)
     for i in range(n_dp):
         got = got + r["dp_in"][i * proj_rows:(i + 1) * proj_rows, :].astype(F32)
     r["d_proj"][...] = got
-    high_sum(1)
-    sums[0].mid()
+    d_high[0].mid2()
     sums[0].finish()
     add_up(0, True)
     r["d_features"][...] = up[...].T.astype(BF)
@@ -707,14 +831,16 @@
         "wanted": ((n_dp, 1, cap), jnp.int32), "asked": ((n_dp, 1, cap), jnp.int32), "asked2": ((n_dp, cap), jnp.int32),
     }
     for l in range(2):
-        for side in ("out", "in"):
-            bufs[f"dh{l}_{side}"] = ((total, 2 * filters), BF)
+        side = math.isqrt(n_dp)
+        bufs[f"dh{l}_out"] = ((side, side, total // n_dp, 2 * filters), BF)
+        for j, spec in enumerate(plane_bufs(side, total // n_dp, filters)):
+            bufs[f"dh{l}_{j}"] = spec
     for i, rows in enumerate((filters, filters, c)):
         for j, spec in enumerate(scatter_bufs(rows, words)):
             if i != 1 or j not in (0, 2):
                 bufs[f"rs{i}_{j}"] = spec
     scratch = [pltpu.VMEM(*spec) for spec in bufs.values()]
-    sems = {"ag": (3, 13), "rs": (3, 10), "dp": (6, n_dp), "raw": (2,)}
+    sems = {"ag": (3, 13), "rs": (3, 10), "dp": (4, n_dp), "ring": (8, 6), "raw": (2,)}
     names = tuple(bufs)
     for name, dims in sems.items():
         names += (name + "_s", name + "_r")
@@ -744,7 +870,7 @@
     return pl.pallas_call(
         kernel, in_specs=[VM] * n, out_specs=[VM] * n,
         out_shape=[jax.ShapeDtypeStruct(a.shape, a.dtype) for a in arrays],
-        compiler_params=pltpu.CompilerParams(vmem_limit_bytes=32 << 20),
+        compiler_params=pltpu.CompilerParams(vmem_limit_bytes=63 << 20),
     )(*arrays)
 
 

time: 180 us -> 154 us (0.86)
  Pallas kernels: 171 us -> 152 us
  local copies, waits for them, and re-layouts: 7.73 us -> 0 us
    pallas_call x1, Pallas kernels: 142 us -> 120 us  [step(): pl.pallas_call(functools.partial(step_kernel, names), in_specs=[pl.BlockS...]
    unnamed x18 -> x0, local copies, waits for them, and re-layouts: 7.73 us -> none
where the time goes in v4:
time: 154 us; the launch traced here: 152 us
  Pallas kernels  152 us (99%)
    pallas_call x1, Pallas kernels, step(): pl.pallas_call(functools.partial(step_kernel, names), in_specs=[pl.BlockS...  120 us
    pallas_call x1, Pallas kernels, encode(): pl.pallas_call(functools.partial(encode_kernel, total, length), grid=(cou...  28.6 us

profile of v4, /device:TPU:1, one launch (start us, length us, event | category | flops | bytes accessed | tf_op | source)
XLA Modules:
  0.0 152.4 jit_solution(4268166273156051307)
XLA Ops:
  0.6 28.6 %shard_map.147.refs_0_ = bf16[256,1024]{1,0:T(8,128)(2,1)} custom-call(s32[50,49152]{1,0:T(8,128)} %bitcast.11, s32[1,1024]{1,0:T(1,128)} %bitcast.17, bf16[16,262]{1,0:T(8,128)(2,1)} %bitcast.16, bf16[112,256]{1,0:T(8,128)(2,1)} %bitcast.13, f32[1,256]{1,0:T(1,128)} %bitcast.18), custom_call_target="tpu_custom_call" | custom-call | tf_op jit(solution)/shard_map/pallas_call | solution.py:143
  29.3 120.2 %shard_map.148 = (bf16[64,8192]{1,0:T(8,128)(2,1)}, bf16[1024,256]{1,0:T(8,128)(2,1)}, f32[2,128,2,256]{3,2,1,0:T(2,128)}, f32[32,256]{1,0:T(8,128)}) custom-call(bf16[256,1024]{1,0:T(8,128)(2,1)} %shard_map.147.refs_0_, bf16[2,2048,2,256]{3,2,1,0:T(2,128)(2,1)} %refs_1_.1, f32[2,2,256]{2,1,0:T(2,128)} %refs_2_.1, bf16[256,512]{1,0:T(8,128)(2,1)} %refs_3_.1, ...), custom_call_target="tpu_custom_call" | custom-call | tf_op jit(solution)/shard_map/pallas_call | solution.py:848
  149.5 2.9 %shard_map.149 = (bf16[64,8192]{1,0:T(8,128)(2,1)}, bf16[1024,256]{1,0:T(8,128)(2,1)}, f32[2,128,2,256]{3,2,1,0:T(2,128)}, f32[32,256]{1,0:T(8,128)}) custom-call(bf16[64,8192]{1,0:T(8,128)(2,1)} %get-tuple-element.12.refs_0_, bf16[1024,256]{1,0:T(8,128)(2,1)} %get-tuple-element.13.refs_1_, f32[2,128,2,256]{3,2,1,0:T(2,128)} %get-tuple-element.14.refs_2_, ...), custom_call_target="tpu_custom_call" | custom-call | tf_op jit(solution)/shard_map/pallas_call | solution.py:870

commit v5 on v4

--- a/solution.py
+++ b/solution.py
@@ -95,7 +95,7 @@
                     jnp.concatenate(halves, axis=0).astype(BF))
             return carry
 
-        lax.fori_loop(0, length, embed, 0)
+        lax.fori_loop(0, length, embed, 0, unroll=5)
 
         base = lax.axis_index("enc") * filters
         width_row = width_of(base + lax.broadcasted_iota(jnp.int32, (128, filters), 1), total)
@@ -139,7 +139,7 @@
     length, count = chars_t.shape
     words = types.shape[1]
     filters = weight.shape[1]
-    block = 4096
+    block = 8192
     return pl.pallas_call(
         functools.partial(encode_kernel, total, length),
         grid=(count // block,),
@@ -597,9 +597,11 @@
     gather = [Gather(place, r["whole0"], filters, r["ag_s"], r["ag_r"], 0),
               Gather(place, r["whole1"], filters, r["ag_s"], r["ag_r"], 1),
               Gather(place, r["grads"], c, r["ag_s"], r["ag_r"], 2)]
-    sums = [Scatter(place, filters, [r[f"rs{0 if j in (0, 2) else i}_{j}"] for j in range(7)], r["rs_s"], r["rs_r"], i)
-            for i in range(2)]
-    proj_sum = Scatter(place, c, [r[f"rs2_{j}"] for j in range(7)], r["rs_s"], r["rs_r"], 2)
+    half = words // 2
+    cols = [slice(0, half), slice(half, words)]
+    sums = [[Scatter(place, filters, [r[f"rs{0 if j in (0, 2) else l}{h}_{j}"] for j in range(7)],
+                     r["rs_s"], r["rs_r"], 2 * l + h) for h in range(2)] for l in range(2)]
+    proj_sum = Scatter(place, c, [r[f"rs2_{j}"] for j in range(7)], r["rs_s"], r["rs_r"], 4)
     high_rows = total // n_dp
     proj_rows = r["proj"].shape[1] // n_dp
 
@@ -651,14 +653,20 @@
             return carry
         lax.fori_loop(0, 2, near, 0)
         gat.forward3()
+        if l == 1:
+            gather[2].forward1()
         add(place.at(2))
         gat.finish_near()
+        if l == 1:
+            gather[2].forward2()
 
         def near_other(i, carry):
             add(place.at(2 * i - 1, True))
             return carry
         lax.fori_loop(0, 2, near_other, 0)
         gat.finish_far()
+        if l == 1:
+            gather[2].forward3()
         add(place.at(2, True))
         for i in range(2):
             r["bcol"][i * filters:(i + 1) * filters, :] = jnp.broadcast_to(
@@ -713,36 +721,36 @@
 
     layer(1, gather[1], r["whole1"], None, owner_part, r["top"])
 
-    top, proj = r["top"], r["proj"]
-    width = r["proj"].shape[1]
-    r["acc"][...] = tn(proj[...], top[...])
-    proj_sum.start(lambda dest: r["acc"][pl.ds(pl.multiple_of(dest * c, c), c), :])
-    gather[2].forward1()
-    gather[2].forward2()
-    gather[2].forward3()
-    gather[2].wait_sib()
-    gather[2].finish_near()
-    gather[2].finish_far()
-    up = r["up"]
-    up[...] = nn(proj[...], r["grads"][...])
-    proj_sum.mid()
-
-    def cell(l):
-        whole = r[f"whole{l}"]
+    top, proj, up, acc = r["top"], r["proj"], r["up"], r["acc"]
+
+    def own(start):
+        return pl.ds(pl.multiple_of(e * filters + start, 32), 32)
+
+    def cell(l, h):
+        whole, at_h = r[f"whole{l}"], cols[h]
 
         def body(at, start):
-            t, g, u = r["t"][l, at, :], r["g"][l, at, :], up[at, :]
-            h = whole[pl.ds(pl.multiple_of(e * filters + start, 32), 32), :].astype(F32)
+            t, g, u = r["t"][l, at, at_h], r["g"][l, at, at_h], up[at, at_h]
+            old = whole[own(start), at_h].astype(F32)
             s = jax.nn.sigmoid(t)
-            r["pre"][l, at, :] = (u * g * (s * (1.0 + t * (1.0 - s)))).astype(BF)
+            r["pre"][l, at, at_h] = (u * g * (s * (1.0 + t * (1.0 - s)))).astype(BF)
             low = pl.ds(pl.multiple_of(filters + start, 32), 32)
-            r["pre"][l, low, :] = (u * (t * s - h) * g * (1.0 - g)).astype(BF)
-            up[at, :] = u * (1.0 - g)
+            r["pre"][l, low, at_h] = (u * (t * s - old) * g * (1.0 - g)).astype(BF)
+            up[at, at_h] = u * (1.0 - g)
         chunks(filters, 32, body)
 
-    def back(l):
+    def back(l, h):
         return lambda dest: nn(
-            r["weight"][l, pl.ds(pl.multiple_of(dest * filters, filters), filters), :], r["pre"][l])
+            r["weight"][l, pl.ds(pl.multiple_of(dest * filters, filters), filters), :],
+            r["pre"][l, :, cols[h]])
+
+    def add_up(l, h):
+        s = sums[l][h]
+        s.finish()
+
+        def body(at, start):
+            up[at, cols[h]] += s.own[at, :] + s.lin[at, :].astype(F32) + s.rin[at, :].astype(F32)
+        chunks(filters, 32, body)
 
     def high_term(l):
         out = r[f"dh{l}_out"]
@@ -757,56 +765,61 @@
         lax.fori_loop(0, side, body, 0)
         d_high[l].start()
 
-    def add_up(l, last):
-        s = sums[l]
-
-        def body(at, start):
-            new = up[at, :] + (s.own[at, :] + s.lin[at, :].astype(F32) + s.rin[at, :].astype(F32))
-            up[at, :] = new
-        chunks(filters, 32, body)
-
     def high_sum(l):
         for i, got in enumerate(d_high[l].finish()):
             r["d_high"][l, :, i, :] = got
 
-    cell(1)
-    sums[1].start(back(1))
+    gather[2].wait_sib()
+    gather[2].finish_near()
+    gather[2].finish_far()
+    for h in range(2):
+        up[:, cols[h]] = nn(proj[...], r["grads"][:, cols[h]])
+        cell(1, h)
+        sums[1][h].start(back(1, h))
+    acc[...] = tn(proj[...], top[...])
+    sums[1][0].mid()
+    proj_sum.start(lambda dest: acc[pl.ds(pl.multiple_of(dest * c, c), c), :])
+    sums[1][1].mid()
+    high_term(1)
+    proj_sum.mid()
+    add_up(1, 0)
+    cell(0, 0)
+    sums[1][0].drain()
+    sums[0][0].start(back(0, 0))
+    d_high[1].mid()
+    add_up(1, 1)
+    cell(0, 1)
+    sums[1][1].drain()
+    high_term(0)
+    sums[0][0].mid()
+    sums[0][1].start(back(0, 1))
     proj_sum.finish()
     r["encoded"][...] = (
         proj_sum.own[...] + proj_sum.lin[...].astype(F32) + proj_sum.rin[...].astype(F32)
         + column(jnp.concatenate([r["pbias"][...], jnp.zeros((1, 128 - c), F32)], axis=1))[:c]).astype(BF)
     owner_pick(r["asked2"], r["encoded"], r["pick_out"])
     picked.start()
-    high_term(1)
-    sums[1].mid()
-    d_high[1].mid()
+    d_high[1].turn()
+    sums[0][1].mid()
+    d_high[0].mid()
+    d_high[1].mid2()
     r["dp_out"][...] = nt(r["grads"][...], top[...]).astype(BF)
     d_proj.start()
-    d_high[1].turn()
-    sums[1].finish()
-    add_up(1, False)
-    cell(0)
-    sums[1].drain()
-    high_term(0)
-    sums[0].start(back(0))
-    d_high[1].mid2()
-    d_high[0].mid()
-    sums[0].mid()
+    d_high[0].turn()
+    high_sum(1)
     picked.wait()
     token_pick(r["slot"], r["pick_in"], r["tokens"])
-    high_sum(1)
-    d_high[0].turn()
+    d_high[0].mid2()
+    add_up(0, 0)
+    add_up(0, 1)
+    r["d_features"][...] = up[...].T.astype(BF)
     d_proj.wait()
     got = jnp.zeros((proj_rows, filters), F32)
     for i in range(n_dp):
         got = got + r["dp_in"][i * proj_rows:(i + 1) * proj_rows, :].astype(F32)
     r["d_proj"][...] = got
-    d_high[0].mid2()
-    sums[0].finish()
-    add_up(0, True)
-    r["d_features"][...] = up[...].T.astype(BF)
     high_sum(0)
-    for x in (asked, slots, picked, d_proj, d_high[0], d_high[1], gather[2], sums[0], proj_sum):
+    for x in (asked, slots, picked, d_proj, d_high[0], d_high[1], gather[2], *sums[0], proj_sum):
         x.drain()
 
 
@@ -835,12 +848,15 @@
         bufs[f"dh{l}_out"] = ((side, side, total // n_dp, 2 * filters), BF)
         for j, spec in enumerate(plane_bufs(side, total // n_dp, filters)):
             bufs[f"dh{l}_{j}"] = spec
-    for i, rows in enumerate((filters, filters, c)):
-        for j, spec in enumerate(scatter_bufs(rows, words)):
-            if i != 1 or j not in (0, 2):
-                bufs[f"rs{i}_{j}"] = spec
+    for l in range(2):
+        for h in range(2):
+            for j, spec in enumerate(scatter_bufs(filters, words // 2)):
+                if l != 1 or j not in (0, 2):
+                    bufs[f"rs{l}{h}_{j}"] = spec
+    for j, spec in enumerate(scatter_bufs(c, words)):
+        bufs[f"rs2_{j}"] = spec
     scratch = [pltpu.VMEM(*spec) for spec in bufs.values()]
-    sems = {"ag": (3, 13), "rs": (3, 10), "dp": (4, n_dp), "ring": (8, 6), "raw": (2,)}
+    sems = {"ag": (3, 13), "rs": (5, 10), "dp": (4, n_dp), "ring": (8, 6), "raw": (2,)}
     names = tuple(bufs)
     for name, dims in sems.items():
         names += (name + "_s", name + "_r")

time: 154 us -> 146 us (0.948)
  Pallas kernels: 152 us -> 145 us
    pallas_call x1, Pallas kernels: 28.6 us -> 22.6 us  [encode(): pl.pallas_call(functools.partial(encode_kernel, total, length), grid=(cou...]
where the time goes in v5:
time: 146 us
  Pallas kernels  145 us (99%)
    pallas_call x1, Pallas kernels, step(): pl.pallas_call(functools.partial(step_kernel, names), in_specs=[pl.BlockS...  120 us
    pallas_call x1, Pallas kernels, encode(): pl.pallas_call(functools.partial(encode_kernel, total, length), grid=(cou...  22.6 us

profile of v5, /device:TPU:1, one launch (start us, length us, event | category | flops | bytes accessed | tf_op | source)
XLA Modules:
  0.0 145.8 jit_solution(9155665209293222503)
XLA Ops:
  0.6 22.6 %shard_map.147.refs_0_ = bf16[256,1024]{1,0:T(8,128)(2,1)} custom-call(s32[50,49152]{1,0:T(8,128)} %bitcast.11, s32[1,1024]{1,0:T(1,128)} %bitcast.17, bf16[16,262]{1,0:T(8,128)(2,1)} %bitcast.16, bf16[112,256]{1,0:T(8,128)(2,1)} %bitcast.13, f32[1,256]{1,0:T(1,128)} %bitcast.18), custom_call_target="tpu_custom_call" | custom-call | tf_op jit(solution)/shard_map/pallas_call | solution.py:143
  23.2 119.8 %shard_map.148 = (bf16[64,8192]{1,0:T(8,128)(2,1)}, bf16[1024,256]{1,0:T(8,128)(2,1)}, f32[2,128,2,256]{3,2,1,0:T(2,128)}, f32[32,256]{1,0:T(8,128)}) custom-call(bf16[256,1024]{1,0:T(8,128)(2,1)} %shard_map.147.refs_0_, bf16[2,2048,2,256]{3,2,1,0:T(2,128)(2,1)} %refs_1_.1, f32[2,2,256]{2,1,0:T(2,128)} %refs_2_.1, bf16[256,512]{1,0:T(8,128)(2,1)} %refs_3_.1, ...), custom_call_target="tpu_custom_call" | custom-call | tf_op jit(solution)/shard_map/pallas_call | solution.py:864
  143.0 2.9 %shard_map.149 = (bf16[64,8192]{1,0:T(8,128)(2,1)}, bf16[1024,256]{1,0:T(8,128)(2,1)}, f32[2,128,2,256]{3,2,1,0:T(2,128)}, f32[32,256]{1,0:T(8,128)}) custom-call(bf16[64,8192]{1,0:T(8,128)(2,1)} %get-tuple-element.12.refs_0_, bf16[1024,256]{1,0:T(8,128)(2,1)} %get-tuple-element.13.refs_1_, f32[2,128,2,256]{3,2,1,0:T(2,128)} %get-tuple-element.14.refs_2_, ...), custom_call_target="tpu_custom_call" | custom-call | tf_op jit(solution)/shard_map/pallas_call | solution.py:886

commit v6 on v5

--- a/solution.py
+++ b/solution.py
@@ -95,7 +95,7 @@
                     jnp.concatenate(halves, axis=0).astype(BF))
             return carry
 
-        lax.fori_loop(0, length, embed, 0, unroll=5)
+        lax.fori_loop(0, length, embed, 0, unroll=10)
 
         base = lax.axis_index("enc") * filters
         width_row = width_of(base + lax.broadcasted_iota(jnp.int32, (128, filters), 1), total)
@@ -518,6 +518,14 @@
     return [((4 * rows, n), BF)] * 3 + [((rows, n), BF)] * 3 + [((rows, n), F32)]
 
 
+WAVES = (
+    ((0, 1), (0, 3), (1, 0), (3, 0)),
+    ((1, 1), (3, 3), (1, 3), (3, 1)),
+    ((0, 2), (2, 0), (2, 2)),
+    ((1, 2), (2, 1), (3, 2), (2, 3)),
+)
+
+
 class Exchange:
     def __init__(self, src, dst, rows, ssem, rsem, index):
         self.src, self.dst, self.rows = src, dst, rows
@@ -528,31 +536,35 @@
     def at(self, ref, i):
         return ref.at[i] if self.rows is None else rows_at(ref, i * self.rows, self.rows)
 
-    def copy(self, j):
-        to = lax.rem(self.me + j, self.n)
-        return send(self.at(self.src, to), self.at(self.dst, self.me),
-                    self.ssem.at[self.index, j], self.rsem.at[self.index, j], dp=to)
+    def peer(self, step):
+        side = math.isqrt(self.n)
+        z, x = self.me // side, lax.rem(self.me, side)
+        return (lax.rem(z + step[0] + side, side) * side + lax.rem(x + step[1] + side, side))
+
+    def sems(self, step):
+        at = step[0] * math.isqrt(self.n) + step[1]
+        return self.ssem.at[self.index, at], self.rsem.at[self.index, at]
+
+    def copy(self, step):
+        to = self.peer(step)
+        return send(self.at(self.src, to), self.at(self.dst, self.me), *self.sems(step), dp=to)
 
     def start(self):
-        def body(j, carry):
-            self.copy(j).start()
-            return carry
-        lax.fori_loop(1, self.n, body, 0)
         self.at(self.dst, self.me)[...] = self.at(self.src, self.me)[...]
+        for group in WAVES:
+            for step in group:
+                self.copy(step).start()
 
     def wait(self):
-        def body(j, carry):
-            came = self.at(self.dst, lax.rem(self.me - j + self.n, self.n))
-            send(came, came, self.ssem.at[self.index, j], self.rsem.at[self.index, j],
-                 dp=lax.rem(self.me + 1, self.n)).wait_recv()
-            return carry
-        lax.fori_loop(1, self.n, body, 0)
+        for group in WAVES:
+            for step in group:
+                came = self.at(self.dst, self.peer((-step[0], -step[1])))
+                send(came, came, *self.sems(step), dp=self.peer((0, 1))).wait_recv()
 
     def drain(self):
-        def body(j, carry):
-            self.copy(j).wait_send()
-            return carry
-        lax.fori_loop(1, self.n, body, 0)
+        for group in WAVES:
+            for step in group:
+                self.copy(step).wait_send()
 
 
 def chunks(count, step, body):
@@ -575,6 +587,8 @@
     c, tokens = r["d_tokens"].shape
     cap = r["requests"].shape[1]
     e = place.at(0)
+    fetch = pltpu.make_async_copy(r["d_tokens"], r["dt"], r["raw_s"].at[2])
+    fetch.start()
     raw = pltpu.make_async_copy(r["weight_in"].at[0], r["raw"], r["raw_s"].at[0])
     raw.start()
     for o in range(n_dp):
@@ -688,6 +702,7 @@
         gat.drain()
 
     n_chunks = tokens // 1024
+    fetch.wait()
     r["sacc"][...] = jnp.zeros_like(r["sacc"])
 
     def slot_part(first, last):
@@ -696,7 +711,7 @@
             slot = r["slot"][:, at]
             hot = one_hot(slot & 255, 256)
             high = slot >> 8
-            d = r["d_tokens"][:, at]
+            d = r["dt"][:, at]
             parts = [d * jnp.where(high == o, 1.0, 0.0).astype(BF) for o in range(n_dp)]
             r["sacc"][...] += nt(jnp.concatenate(parts, axis=0), hot)
             return carry
@@ -786,6 +801,12 @@
     cell(0, 0)
     sums[1][0].drain()
     sums[0][0].start(back(0, 0))
+    proj_sum.finish()
+    r["encoded"][...] = (
+        proj_sum.own[...] + proj_sum.lin[...].astype(F32) + proj_sum.rin[...].astype(F32)
+        + column(jnp.concatenate([r["pbias"][...], jnp.zeros((1, 128 - c), F32)], axis=1))[:c]).astype(BF)
+    owner_pick(r["asked2"], r["encoded"], r["pick_out"])
+    picked.start()
     d_high[1].mid()
     add_up(1, 1)
     cell(0, 1)
@@ -793,22 +814,18 @@
     high_term(0)
     sums[0][0].mid()
     sums[0][1].start(back(0, 1))
-    proj_sum.finish()
-    r["encoded"][...] = (
-        proj_sum.own[...] + proj_sum.lin[...].astype(F32) + proj_sum.rin[...].astype(F32)
-        + column(jnp.concatenate([r["pbias"][...], jnp.zeros((1, 128 - c), F32)], axis=1))[:c]).astype(BF)
-    owner_pick(r["asked2"], r["encoded"], r["pick_out"])
-    picked.start()
     d_high[1].turn()
     sums[0][1].mid()
     d_high[0].mid()
     d_high[1].mid2()
+    picked.wait()
+    token_pick(r["slot"], r["pick_in"], r["tok"])
+    store = pltpu.make_async_copy(r["tok"], r["tokens"], r["raw_s"].at[3])
+    store.start()
     r["dp_out"][...] = nt(r["grads"][...], top[...]).astype(BF)
     d_proj.start()
     d_high[0].turn()
     high_sum(1)
-    picked.wait()
-    token_pick(r["slot"], r["pick_in"], r["tokens"])
     d_high[0].mid2()
     add_up(0, 0)
     add_up(0, 1)
@@ -819,6 +836,7 @@
         got = got + r["dp_in"][i * proj_rows:(i + 1) * proj_rows, :].astype(F32)
     r["d_proj"][...] = got
     high_sum(0)
+    store.wait()
     for x in (asked, slots, picked, d_proj, d_high[0], d_high[1], gather[2], *sums[0], proj_sum):
         x.drain()
 
@@ -840,6 +858,7 @@
         "pick_out": ((n_dp * c, cap), BF), "pick_in": ((n_dp * c, cap), BF),
         "row": ((c, words), BF), "encoded": ((c, words), BF),
         "dp_out": ((width, filters), BF), "dp_in": ((width, filters), BF),
+        "dt": ((c, tokens), BF), "tok": ((c, tokens), BF),
         "weight": ((2, total, 2 * filters), BF), "raw": ((total, 2, filters), BF),
         "wanted": ((n_dp, 1, cap), jnp.int32), "asked": ((n_dp, 1, cap), jnp.int32), "asked2": ((n_dp, cap), jnp.int32),
     }
@@ -856,14 +875,14 @@
     for j, spec in enumerate(scatter_bufs(c, words)):
         bufs[f"rs2_{j}"] = spec
     scratch = [pltpu.VMEM(*spec) for spec in bufs.values()]
-    sems = {"ag": (3, 13), "rs": (5, 10), "dp": (4, n_dp), "ring": (8, 6), "raw": (2,)}
+    sems = {"ag": (3, 13), "rs": (5, 10), "dp": (4, n_dp), "ring": (8, 6), "raw": (4,)}
     names = tuple(bufs)
     for name, dims in sems.items():
         names += (name + "_s", name + "_r")
         scratch += [pltpu.SemaphoreType.DMA(dims)] * 2
     return pl.pallas_call(
         functools.partial(step_kernel, names),
-        in_specs=[pl.BlockSpec(memory_space=pl.ANY) if x == "weight_in" else VM for x in INPUTS], out_specs=[VM] * len(OUTPUTS),
+        in_specs=[pl.BlockSpec(memory_space=pl.ANY) if x in ("weight_in", "d_tokens") else VM for x in INPUTS], out_specs=[pl.BlockSpec(memory_space=pl.ANY) if x == "tokens" else VM for x in OUTPUTS],
         out_shape=[
             jax.ShapeDtypeStruct((c, tokens), BF),
             jax.ShapeDtypeStruct((words, filters), BF),

time: 146 us -> 147 us (level); the launches traced: 146 us -> 145 us
  no operation moved by 1% of the time
where the time goes in v6:
time: 147 us; the launch traced here: 145 us
  Pallas kernels  144 us (98%)
    pallas_call x1, Pallas kernels, step(): pl.pallas_call(functools.partial(step_kernel, names), in_specs=[pl.BlockS...  119 us
    pallas_call x1, Pallas kernels, encode(): pl.pallas_call(functools.partial(encode_kernel, total, length), grid=(cou...  22.2 us

profile of v6, /device:TPU:1, one launch (start us, length us, event | category | flops | bytes accessed | tf_op | source)
XLA Modules:
  0.0 145.0 jit_solution(2674340415496053304)
XLA Ops:
  0.6 22.2 %shard_map.147.refs_0_ = bf16[256,1024]{1,0:T(8,128)(2,1)} custom-call(s32[50,49152]{1,0:T(8,128)} %bitcast.11, s32[1,1024]{1,0:T(1,128)} %bitcast.17, bf16[16,262]{1,0:T(8,128)(2,1)} %bitcast.16, bf16[112,256]{1,0:T(8,128)(2,1)} %bitcast.13, f32[1,256]{1,0:T(1,128)} %bitcast.18), custom_call_target="tpu_custom_call" | custom-call | tf_op jit(solution)/shard_map/pallas_call | solution.py:143
  22.8 119.3 %shard_map.148 = (bf16[64,8192]{1,0:T(8,128)(2,1)}, bf16[1024,256]{1,0:T(8,128)(2,1)}, f32[2,128,2,256]{3,2,1,0:T(2,128)}, f32[32,256]{1,0:T(8,128)}) custom-call(bf16[256,1024]{1,0:T(8,128)(2,1)} %shard_map.147.refs_0_, bf16[2,2048,2,256]{3,2,1,0:T(2,128)(2,1)} %refs_1_.1, f32[2,2,256]{2,1,0:T(2,128)} %refs_2_.1, bf16[256,512]{1,0:T(8,128)(2,1)} %refs_3_.1, ...), custom_call_target="tpu_custom_call" | custom-call | tf_op jit(solution)/shard_map/pallas_call | solution.py:883
  142.1 2.9 %shard_map.149 = (bf16[64,8192]{1,0:T(8,128)(2,1)}, bf16[1024,256]{1,0:T(8,128)(2,1)}, f32[2,128,2,256]{3,2,1,0:T(2,128)}, f32[32,256]{1,0:T(8,128)}) custom-call(bf16[64,8192]{1,0:T(8,128)(2,1)} %get-tuple-element.12.refs_0_, bf16[1024,256]{1,0:T(8,128)(2,1)} %get-tuple-element.13.refs_1_, f32[2,128,2,256]{3,2,1,0:T(2,128)} %get-tuple-element.14.refs_2_, ...), custom_call_target="tpu_custom_call" | custom-call | tf_op jit(solution)/shard_map/pallas_call | solution.py:905
